TPU v7x, 256 devices: a whole 4x4x8 slice. The times are simulated.
256 devices in a mesh: gx: 8 (over z), gy: 16 (over y, x), gz: 2 (over core).
Axes of the slice: x: 4, y: 4, z: 8, core: 2. Of those that a mesh axis runs over, the one named last changes fastest.
Arguments:
- adjoint_rhs: float32 [2, 128, 256, 2048], P(None, 'gx', 'gy', 'gz'), may hold values from -8 to 8
- conductance: float32 [128, 256, 2048], P('gx', 'gy', 'gz'), may hold values from 0.2 to 5
- phase: int32 [128, 256, 2048], P('gx', 'gy', 'gz'), may hold values from 0 to 2
- particle_rhs: float32 [1200, 8192], P(None, ('gx', 'gy', 'gz')), may hold values from -8 to 8
- diffusion_rate: float32 [8, 8192], P(None, ('gx', 'gy', 'gz')), may hold values from 0.2 to 5
- exchange_rate: float32 [8, 8192], P(None, ('gx', 'gy', 'gz')), may hold values from 0.3 to 3
- record_voxel: int32 [8, 16, 2, 3, 512], P('gx', 'gy', 'gz'), may hold values from 0 to 262143, as said below
- record_slot: int32 [8, 16, 2, 3, 512], P('gx', 'gy', 'gz'), may hold values from 0 to 255, as said below
- record_weight: float32 [8, 16, 2, 3, 512], P('gx', 'gy', 'gz'), may hold values from 0 to 1, as said below
Outputs:
- voxel_adjoint: float32 [2, 128, 256, 2048], P(None, 'gx', 'gy', 'gz')
- shell_adjoint: float32 [1200, 8192], P(None, ('gx', 'gy', 'gz'))
Inputs may be any that keep to these rules, and one draw needn't show every extreme that they name: `record_voxel`: index within the brick of a voxel; for block 0 (2) a voxel among the first (last) 4 layers along the second dimension, at least one layer. `record_slot`: class times 32 plus column on the brick named by the fourth index. `record_weight`: zero in unused slots and in blocks whose brick lies outside the grid; the used slots of each block of 512 come first; every brick fills all 512 slots of one of its blocks.
All inputs are finite; a program needn't handle non-finite values.
Results may differ from a plain program's by a relative error of at most 0.0001.
Values sent between devices are 32-bit elements; how exact they have to be, the bound alone decides.
A program may use at most 128 MiB of HBM per device.

v0:
```python
import jax
import jax.numpy as jnp
from jax import lax
from jax.sharding import PartitionSpec as P

ITERS = 4


shell_counts = (64, 80, 96, 128, 160, 192, 224, 256)
conduct_potential = (1.0, 0.1, 0.5)
conduct_salt = (1.0, 0.05, 0.3)
mass_potential = (1.0, 0.5, 0.8)
mass_salt = (1.0, 2.0, 1.5)
coupling_weights = (1.0, 0.5)


def extended(x, sides, width):
    for axis, dim in sides:
        peers, length = (lax.axis_size(axis), x.shape[dim])
        up = [(i, (i + 1) % peers) for i in range(peers - 1)]
        down = [(j, i) for i, j in up]
        last = lax.slice_in_dim(x, length - width, length, axis=dim)
        leading = lax.slice_in_dim(x, 0, width, axis=dim)
        before = lax.ppermute(last, axis, up)
        after = lax.ppermute(leading, axis, down)
        x = jnp.concatenate([before, x, after], axis=dim)
    return x


def phase_value(phase, values):
    return jnp.where(phase == 0, values[0], jnp.where(phase == 1, values[1], values[2]))


def neighbours(padded):
    return [
        padded[:, 2:, 1:-1, 1:-1],
        padded[:, :-2, 1:-1, 1:-1],
        padded[:, 1:-1, 2:, 1:-1],
        padded[:, 1:-1, :-2, 1:-1],
        padded[:, 1:-1, 1:-1, 2:],
        padded[:, 1:-1, 1:-1, :-2],
    ]


def shell_geometry(count):
    faces = jnp.arange(count + 1).astype(jnp.float32)
    area = jnp.where(faces < count, (faces / count) ** 2, 0.0)
    shells = jnp.arange(count).astype(jnp.float32)
    volume = (3.0 * shells * shells + 3.0 * shells + 1.0) / (3.0 * count * count)
    return (area, volume)


def particle_update(block, rhs_block, rate, gamma, surf, area, volume, diagonal):
    scaled = block / volume[:, None]
    padded = jnp.pad(scaled, ((1, 1), (0, 0)))
    inner = area[1:, None] * padded[2:] + area[:-1, None] * padded[:-2]
    numer = rhs_block + rate[None, :] * inner
    numer = numer.at[-1].add(gamma * surf)
    return numer / diagonal


def shards(
    adjoint_rhs,
    conductance,
    phase,
    particle_rhs,
    diffusion_rate,
    exchange_rate,
    record_voxel,
    record_slot,
    record_weight,
):
    fields, size_x, size_y, size_z = adjoint_rhs.shape
    cells = size_x * size_y * size_z
    classes, columns = diffusion_rate.shape
    per_row = classes * columns
    kappa = conductance[None] * jnp.stack(
        [phase_value(phase, conduct_potential), phase_value(phase, conduct_salt)]
    )
    mass = jnp.stack([phase_value(phase, mass_potential), phase_value(phase, mass_salt)])
    padded_k = extended(kappa, (("gx", 1), ("gy", 2), ("gz", 3)), 1)
    coefs = [2.0 * kappa * other / (kappa + other) for other in neighbours(padded_k)]
    voxel_index = record_voxel[0, 0, 0]
    slot_index = record_slot[0, 0, 0]
    weight = record_weight[0, 0, 0]
    voxel_flat = voxel_index.reshape(-1)
    weight_flat = weight.reshape(-1)
    voxel_weight = (
        jnp.zeros((cells,), jnp.float32)
        .at[voxel_flat]
        .add(weight_flat)
        .reshape(size_x, size_y, size_z)
    )
    coupling = jnp.array(coupling_weights, jnp.float32)[:, None, None, None]
    diag_x = mass + coupling * voxel_weight[None] + sum(coefs)
    slot_rims = extended(slot_index, (("gy", 0),), 1)
    weight_rims = extended(weight, (("gy", 0),), 1)
    arrived_slot = jnp.stack([slot_rims[0], slot_index[1], slot_rims[4]])
    arrived_weight = jnp.stack([weight_rims[0], weight[1], weight_rims[4]])
    arrived_flat = arrived_slot.reshape(-1)
    particle_weight = (
        jnp.zeros((per_row,), jnp.float32).at[arrived_flat].add(arrived_weight.reshape(-1))
    )
    particle_weight = particle_weight.reshape(classes, columns)
    starts = [sum(shell_counts[:index]) for index in range(len(shell_counts))]
    geometry = []
    blocks = []
    for index, count in enumerate(shell_counts):
        area, volume = shell_geometry(count)
        diagonal = 1.0 + diffusion_rate[index][None, :] * ((area[1:] + area[:-1]) / volume)[:, None]
        diagonal = diagonal.at[-1].add(
            exchange_rate[index]
            * (coupling_weights[0] + coupling_weights[1])
            * particle_weight[index]
        )
        geometry.append((area, volume, diagonal))
        blocks.append(particle_rhs[starts[index] : starts[index] + count] / diagonal)
    voxel_adj = adjoint_rhs / diag_x
    for step in range(ITERS):
        last = jnp.stack([block[-1] for block in blocks]).reshape(-1)
        flat_x = voxel_adj.reshape(fields, cells)
        mixed = coupling_weights[0] * flat_x[0] + coupling_weights[1] * flat_x[1]
        picked = weight * mixed[voxel_index]
        answers = last[arrived_slot]
        both_rims = extended(jnp.stack([picked, answers]), (("gy", 1),), 1)
        arrived_vals = jnp.stack([both_rims[0, 0], picked[1], both_rims[0, 4]])
        returned = jnp.stack([both_rims[1, 0], answers[1], both_rims[1, 4]])
        surf = jnp.zeros((per_row,), jnp.float32).at[arrived_flat].add(arrived_vals.reshape(-1))
        surf = surf.reshape(classes, columns)
        back = (
            jnp.zeros((cells,), jnp.float32)
            .at[voxel_flat]
            .add((weight * returned).reshape(-1))
            .reshape(size_x, size_y, size_z)
        )
        padded = extended(voxel_adj, (("gx", 1), ("gy", 2), ("gz", 3)), 1)
        near_sum = sum((coef * other for coef, other in zip(coefs, neighbours(padded))))
        new_x = (adjoint_rhs + near_sum + coupling * back[None]) / diag_x
        new_blocks = []
        for index, count in enumerate(shell_counts):
            area, volume, diagonal = geometry[index]
            new_blocks.append(
                particle_update(
                    blocks[index],
                    particle_rhs[starts[index] : starts[index] + count],
                    diffusion_rate[index],
                    exchange_rate[index],
                    surf[index],
                    area,
                    volume,
                    diagonal,
                )
            )
        voxel_adj = new_x
        blocks = new_blocks
    return (voxel_adj, jnp.concatenate(blocks, axis=0))


def solution(mesh):
    in_specs = (
        P(None, "gx", "gy", "gz"),
        P("gx", "gy", "gz"),
        P("gx", "gy", "gz"),
        P(None, ("gx", "gy", "gz")),
        P(None, ("gx", "gy", "gz")),
        P(None, ("gx", "gy", "gz")),
        P("gx", "gy", "gz", None, None),
        P("gx", "gy", "gz", None, None),
        P("gx", "gy", "gz", None, None),
    )
    out_specs = (P(None, "gx", "gy", "gz"), P(None, ("gx", "gy", "gz")))
    return jax.shard_map(shards, mesh=mesh, in_specs=in_specs, out_specs=out_specs, check_vma=False)
```

profile of v0, /device:TPU:104, one launch (start us, length us, event | category | flops | bytes accessed | tf_op | source)
XLA Modules:
  0.0 770.8 jit_solution(12133322252482856851)
XLA Ops:
  1.9 3.4 collective-permute-start.12
  5.3 4.6 collective-permute-start.13
  13.1 6.0 collective-permute-start.15
  23.2 5.0 collective-permute-start.1
  61.9 9.7 %scatter_custom_fusion = f32[262144]{0:T(1024)} fusion(s32[1536]{0:T(1024)} %fusion.197, f32[1536]{0:T(1024)S(1)} %reshape.1614, f32[]{:T(128)} %constant.948.clone.1), kind=kCustom, calls=%fused_computation.197 | custom fusion | flops 1536 | bytes 1049088 | tf_op jit(solution)/shard_map/scatter-add | solution.py:91
  82.5 11.8 %scatter_custom_fusion.1 = f32[256]{0:T(256)} fusion(s32[1536]{0:T(1024)} %fusion.199, f32[1536]{0:T(1024)} %reshape.1622, f32[]{:T(128)} %constant.948.clone.1), kind=kCustom, calls=%fused_computation.692 | custom fusion | flops 1536 | bytes 1536 | tf_op jit(solution)/shard_map/scatter-add | solution.py:102
  135.8 3.9 collective-permute-start.3
  141.6 3.9 collective-permute-done.3
  151.3 9.4 %gather_fusion.1 = f32[1536]{0:T(1024)S(1)} fusion(f32[256]{0:T(256)S(1)} %reshape.1506, s32[2048]{0:T(1024)S(1)} %pad_clamp_fusion), kind=kCustom, calls=%fused_computation.1 | custom fusion | bytes 18432 | tf_op jit(solution)/shard_map/gather | solution.py:124
  160.9 10.2 %fusion.235 = f32[2,16,16,1024]{3,2,1,0:T(8,128)S(1)} fusion(f32[2,16,16,1024]{3,2,1,0:T(8,128)} %param.90, f32[16,16,1024]{2,1,0:T(8,128)} %mul.1378, f32[2]{0:T(128)S(1)} %copy-done.103, f32[1,16,16,1024]{3,2,1,0:T(8,128)} %get-tuple-element.525, f32[1,16,16,1024]{3,2,1,0:T(8,128)S(1)} %get-tuple-element.524, ...), kind=kLoop, calls=%fused_computation.696 | loop fusion | flops 24641536 | bytes 9999432 | tf_op jit(solution)/shard_map/div | solution.py:118
  172.4 8.4 %gather_fusion = f32[1536]{0:T(1024)S(1)} fusion(f32[262144]{0:T(1024)S(1)} %bitcast.325, s32[2048]{0:T(1024)S(1)} %copy-done.68), kind=kCustom, calls=%fused_computation | custom fusion | bytes 18432 | tf_op jit(solution)/shard_map/gather | solution.py:123
  184.4 5.3 collective-permute-start.7
  191.6 6.0 collective-permute-start.17
  200.5 6.4 collective-permute-start.8
  211.7 6.1 collective-permute-done.9
  220.6 4.6 collective-permute-start.11
  225.3 10.1 %scatter_custom_fusion.2 = f32[262144]{0:T(1024)} fusion(s32[1536]{0:T(1024)} %fusion.197, f32[1536]{0:T(1024)S(1)} %mul.1458, f32[]{:T(128)} %constant.948.clone.1), kind=kCustom, calls=%fused_computation.195 | custom fusion | flops 1536 | bytes 1049088 | tf_op jit(solution)/shard_map/scatter-add | solution.py:133
  237.8 19.2 %fusion.46 = f32[2,16,16,1024]{3,2,1,0:T(8,128)S(1)} fusion(f32[2,16,16,1024]{3,2,1,0:T(8,128)} %param.90, f32[2,18,18,1]{3,2,1,0:T(8,128)} %collective-permute-done.11, f32[2,18,1,1024]{3,2,1,0:T(1,128)} %copy-done.47, f32[2,18,1,1024]{3,2,1,0:T(1,128)} %copy-done.49, f32[2,1,16,1024]{3,2,1,0:T(8,128)} %copy-done.57, f32[2,16,16,1024]{3,2,1,0:T(8,128)} %copy-done.6, ...), kind=kLoop, calls=%fused_computation.119 | loop fusion | flops 41418752 | bytes 13707400 | tf_op jit(solution)/shard_map/div | solution.py:138
  258.4 12.0 %gather_fusion.2 = f32[1536]{0:T(1024)} fusion(f32[262144]{0:T(1024)S(1)} %bitcast.326, s32[2048]{0:T(1024)} %pad_clamp_fusion.1), kind=kCustom, calls=%fused_computation.2 | custom fusion | bytes 18432 | tf_op jit(solution)/shard_map/gather | solution.py:123
  274.6 11.3 %scatter_custom_fusion.3 = f32[256]{0:T(256)S(1)} fusion(s32[1536]{0:T(1024)} %fusion.199, f32[1536]{0:T(1024)S(1)} %reshape.1638, f32[]{:T(128)} %constant.948.clone.1), kind=kCustom, calls=%fused_computation.690 | custom fusion | flops 1536 | bytes 1536 | tf_op jit(solution)/shard_map/scatter-add | solution.py:128
  318.0 3.9 collective-permute-start.18
  334.3 9.4 %gather_fusion.3 = f32[1536]{0:T(1024)S(1)} fusion(f32[256]{0:T(256)S(1)} %reshape.1516, s32[2048]{0:T(1024)S(1)} %copy-done.70), kind=kCustom, calls=%fused_computation.3 | custom fusion | bytes 18432 | tf_op jit(solution)/shard_map/gather | solution.py:124
  348.6 6.0 collective-permute-start.25
  357.2 11.3 %scatter_custom_fusion.5 = f32[256]{0:T(256)S(1)} fusion(s32[1536]{0:T(1024)} %fusion.199, f32[1536]{0:T(1024)S(1)} %reshape.1654, f32[]{:T(128)} %constant.948.clone.1), kind=kCustom, calls=%fused_computation.688 | custom fusion | flops 1536 | bytes 1536 | tf_op jit(solution)/shard_map/scatter-add | solution.py:128
  412.5 6.3 collective-permute-start.20
  422.1 6.3 collective-permute-done.21
  431.9 4.6 collective-permute-start.23
  437.3 12.8 %gather_fusion.5 = f32[1536]{0:T(1024)} fusion(f32[256]{0:T(256)S(1)} %reshape.1526, s32[2048]{0:T(1024)S(1)} %copy-done.71), kind=kCustom, calls=%fused_computation.5 | custom fusion | bytes 18432 | tf_op jit(solution)/shard_map/gather | solution.py:124
  455.4 9.7 %scatter_custom_fusion.4 = f32[262144]{0:T(1024)} fusion(s32[1536]{0:T(1024)} %fusion.197, f32[1536]{0:T(1024)} %mul.1519, f32[]{:T(128)} %constant.948.clone.1), kind=kCustom, calls=%fused_computation.193 | custom fusion | flops 1536 | bytes 1049088 | tf_op jit(solution)/shard_map/scatter-add | solution.py:133
  467.5 19.2 %fusion.32 = f32[2,16,16,1024]{3,2,1,0:T(8,128)S(1)} fusion(f32[2,16,16,1024]{3,2,1,0:T(8,128)} %param.90, f32[2,18,18,1]{3,2,1,0:T(8,128)} %collective-permute-done.23, f32[2,18,1,1024]{3,2,1,0:T(1,128)} %copy-done.45, f32[2,18,1,1024]{3,2,1,0:T(1,128)} %copy-done.46, f32[2,1,16,1024]{3,2,1,0:T(8,128)} %collective-permute-done.18, ...), kind=kLoop, calls=%fused_computation.87 | loop fusion | flops 41418752 | bytes 13707400 | tf_op jit(solution)/shard_map/div | solution.py:138
  488.0 11.9 %gather_fusion.4 = f32[1536]{0:T(1024)} fusion(f32[262144]{0:T(1024)S(1)} %bitcast.327, s32[2048]{0:T(1024)} %pad_clamp_fusion.1), kind=kCustom, calls=%fused_computation.4 | custom fusion | bytes 18432 | tf_op jit(solution)/shard_map/gather | solution.py:123
  511.5 6.0 collective-permute-start.33
  520.2 4.7 collective-permute-start.28
  528.2 6.3 collective-permute-done.29
  537.4 4.6 collective-permute-start.31
  545.3 9.9 %scatter_custom_fusion.6 = f32[262144]{0:T(1024)} fusion(s32[1536]{0:T(1024)} %fusion.197, f32[1536]{0:T(1024)} %mul.1564, f32[]{:T(128)} %constant.948.clone.1), kind=kCustom, calls=%fused_computation.191 | custom fusion | flops 1536 | bytes 1049088 | tf_op jit(solution)/shard_map/scatter-add | solution.py:133
  557.5 19.2 %fusion.18 = f32[2,16,16,1024]{3,2,1,0:T(8,128)S(1)} fusion(f32[2,16,16,1024]{3,2,1,0:T(8,128)} %param.90, f32[2,18,18,1]{3,2,1,0:T(8,128)} %collective-permute-done.31, f32[2,18,1,1024]{3,2,1,0:T(1,128)} %copy-done.48, f32[2,18,1,1024]{3,2,1,0:T(1,128)} %copy-done.50, f32[2,1,16,1024]{3,2,1,0:T(8,128)} %copy-done.58, f32[2,16,16,1024]{3,2,1,0:T(8,128)} %copy-done.4, ...), kind=kLoop, calls=%fused_computation.55 | loop fusion | flops 41418752 | bytes 13707400 | tf_op jit(solution)/shard_map/div | solution.py:138
  578.2 12.0 %gather_fusion.6 = f32[1536]{0:T(1024)} fusion(f32[262144]{0:T(1024)S(1)} %bitcast.324, s32[2048]{0:T(1024)} %pad_clamp_fusion.1), kind=kCustom, calls=%fused_computation.6 | custom fusion | bytes 18432 | tf_op jit(solution)/shard_map/gather | solution.py:123
  593.6 11.3 %scatter_custom_fusion.7 = f32[256]{0:T(256)S(1)} fusion(s32[1536]{0:T(1024)} %fusion.199, f32[1536]{0:T(1024)S(1)} %reshape.1670, f32[]{:T(128)} %constant.948.clone.1), kind=kCustom, calls=%fused_computation.686 | custom fusion | flops 1536 | bytes 1536 | tf_op jit(solution)/shard_map/scatter-add | solution.py:128
  634.7 9.7 %gather_fusion.7 = f32[1536]{0:T(1024)S(1)} fusion(f32[256]{0:T(256)S(1)} %reshape.1536, s32[2048]{0:T(1024)} %copy-done.69), kind=kCustom, calls=%fused_computation.7 | custom fusion | bytes 18432 | tf_op jit(solution)/shard_map/gather | solution.py:124
  647.5 3.9 collective-permute-start.34
  663.7 6.0 collective-permute-start.41
  671.7 11.3 %scatter_custom_fusion.9 = f32[256]{0:T(256)S(1)} fusion(s32[1536]{0:T(1024)} %fusion.199, f32[1536]{0:T(1024)S(1)} %reshape.1686, f32[]{:T(128)} %constant.948.clone.1), kind=kCustom, calls=%fused_computation.684 | custom fusion | flops 1536 | bytes 1536 | tf_op jit(solution)/shard_map/scatter-add | solution.py:128
  686.5 6.3 collective-permute-start.36
  696.2 6.3 collective-permute-done.37
  705.3 4.6 collective-permute-start.39
  736.5 9.7 %scatter_custom_fusion.8 = f32[262144]{0:T(1024)} fusion(s32[1536]{0:T(1024)} %fusion.197, f32[1536]{0:T(1024)} %mul.1609, f32[]{:T(128)} %constant.948.clone.1), kind=kCustom, calls=%fused_computation.189 | custom fusion | flops 1536 | bytes 1049088 | tf_op jit(solution)/shard_map/scatter-add | solution.py:133
  750.2 20.1 %fusion.4 = f32[2,16,16,1024]{3,2,1,0:T(8,128)} fusion(f32[2,16,16,1024]{3,2,1,0:T(8,128)} %param.90, f32[2,18,18,1]{3,2,1,0:T(8,128)} %collective-permute-done.39, f32[2,18,1,1024]{3,2,1,0:T(1,128)} %copy-done.43, f32[2,18,1,1024]{3,2,1,0:T(1,128)} %copy-done.44, f32[2,1,16,1024]{3,2,1,0:T(8,128)} %copy-done.54, f32[2,16,16,1024]{3,2,1,0:T(8,128)} %copy-done, ...), kind=kLoop, calls=%fused_computation.23 | loop fusion | flops 41418752 | bytes 13707400 | tf_op jit(solution)/shard_map/div | solution.py:138
  (652 shorter events, 356.5 us)
Async XLA Ops:
  1.9 72.1 %collective-permute-start.12 = (s32[1,512]{1,0:T(1,128)}, s32[1,512]{1,0:T(1,128)}, u32[]{:S(2)}, u32[]{:S(2)}) collective-permute-start(s32[1,512]{1,0:T(1,128)} %get-tuple-element.539), channel_id=1, source_target_pairs={{0,2},{2,4},{4,6},{6,8},{8,10},{10,12},{12,14},{14,16},{16,18},{18... | collective-permute-start | bytes 6152 | tf_op jit(solution)/shard_map/ppermute | solution.py:24
  5.3 70.6 %collective-permute-start.13 = (s32[1,512]{1,0:T(1,128)}, s32[1,512]{1,0:T(1,128)}, u32[]{:S(2)}, u32[]{:S(2)}) collective-permute-start(s32[1,512]{1,0:T(1,128)} %get-tuple-element.540), channel_id=1, source_target_pairs={{2,0},{4,2},{6,4},{8,6},{10,8},{12,10},{14,12},{16,14},{18,16},{20... | collective-permute-start | bytes 6152 | tf_op jit(solution)/shard_map/ppermute | solution.py:25
  11.2 68.7 %collective-permute-start.14 = (f32[1,512]{1,0:T(1,128)}, f32[1,512]{1,0:T(1,128)}, u32[]{:S(2)}, u32[]{:S(2)}) collective-permute-start(f32[1,512]{1,0:T(1,128)} %get-tuple-element.542), channel_id=1, source_target_pairs={{0,2},{2,4},{4,6},{6,8},{8,10},{10,12},{12,14},{14,16},{16,18},{18... | collective-permute-start | bytes 6152 | tf_op jit(solution)/shard_map/ppermute | solution.py:24
  13.1 66.8 %collective-permute-start.15 = (f32[1,512]{1,0:T(1,128)}, f32[1,512]{1,0:T(1,128)}, u32[]{:S(2)}, u32[]{:S(2)}) collective-permute-start(f32[1,512]{1,0:T(1,128)} %get-tuple-element.544), channel_id=1, source_target_pairs={{2,0},{4,2},{6,4},{8,6},{10,8},{12,10},{14,12},{16,14},{18,16},{20... | collective-permute-start | bytes 6152 | tf_op jit(solution)/shard_map/ppermute | solution.py:25
  22.1 138.7 %copy-start.8 = (f32[1,16,16,1024]{3,2,1,0:T(8,128)}, f32[1,16,16,1024]{3,2,1,0:T(8,128)S(1)}, u32[]{:S(2)}) copy-start(f32[1,16,16,1024]{3,2,1,0:T(8,128)S(1)} %get-tuple-element.524) | copy-start | bytes 3145732
  23.2 110.3 %collective-permute-start.1 = (f32[2,1,16,1024]{3,2,1,0:T(8,128)}, f32[2,1,16,1024]{3,2,1,0:T(8,128)S(1)}, u32[]{:S(2)}, u32[]{:S(2)}) collective-permute-start(f32[2,1,16,1024]{3,2,1,0:T(8,128)} %get-tuple-element.521), channel_id=1, source_target_pairs={{0,32},{32,64},{64,96},{96,128},{128,160},{160,192},{192,224},{1,3... | collective-permute-start | bytes 393224 | tf_op jit(solution)/shard_map/ppermute | solution.py:24
  35.3 95.4 %copy-start.77 = (f32[256]{0:T(256)}, f32[256]{0:T(256)S(1)}, u32[]{:S(2)}) copy-start(f32[256]{0:T(256)S(1)} %get-tuple-element.609) | copy-start | bytes 3076
  74.0 59.5 %collective-permute-start = (f32[2,1,16,1024]{3,2,1,0:T(8,128)}, f32[2,1,16,1024]{3,2,1,0:T(8,128)S(1)}, u32[]{:S(2)}, u32[]{:S(2)}) collective-permute-start(f32[2,1,16,1024]{3,2,1,0:T(8,128)} %get-tuple-element.522), channel_id=1, source_target_pairs={{32,0},{64,32},{96,64},{128,96},{160,128},{192,160},{224,192},{33,... | collective-permute-start | bytes 393224 | tf_op jit(solution)/shard_map/ppermute | solution.py:25
  133.9 7.6 collective-permute-start.2
  135.8 9.7 %collective-permute-start.3 = (f32[2,18,1,1024]{3,1,2,0:T(8,128)S(1)}, f32[2,18,1,1024]{3,1,2,0:T(8,128)S(1)}, u32[]{:S(2)}, u32[]{:S(2)}) collective-permute-start(f32[2,18,1,1024]{3,1,2,0:T(8,128)S(1)} %copy.91), channel_id=1, source_target_pairs={{0,2},{2,4},{4,6},{6,8},{8,10},{10,12},{12,14},{14,16},{16,18},{18... | collective-permute-start | bytes 442376 | tf_op jit(solution)/shard_map/ppermute | solution.py:24
  147.6 13.2 %collective-permute-start.5 = (f32[2,18,18,1]{3,2,1,0:T(8,128)}, f32[2,18,18,1]{3,2,1,0:T(8,128)}, u32[]{:S(2)}, u32[]{:S(2)}) collective-permute-start(f32[2,18,18,1]{3,2,1,0:T(8,128)} %get-tuple-element.501), channel_id=1, source_target_pairs={{0,1},{2,3},{4,5},{6,7},{8,9},{10,11},{12,13},{14,15},{16,17},{18,... | collective-permute-start | bytes 7784 | tf_op jit(solution)/shard_map/ppermute | solution.py:24
  149.6 11.2 %collective-permute-start.4 = (f32[2,18,18,1]{3,2,1,0:T(8,128)}, f32[2,18,18,1]{3,2,1,0:T(8,128)}, u32[]{:S(2)}, u32[]{:S(2)}) collective-permute-start(f32[2,18,18,1]{3,2,1,0:T(8,128)} %get-tuple-element.502), channel_id=1, source_target_pairs={{1,0},{3,2},{5,4},{7,6},{9,8},{11,10},{13,12},{15,14},{17,16},{19,... | collective-permute-start | bytes 7784 | tf_op jit(solution)/shard_map/ppermute | solution.py:25
  180.9 16.8 %collective-permute-start.16 = (f32[2,1,512]{2,0,1:T(2,128)S(1)}, f32[2,1,512]{2,0,1:T(2,128)S(1)}, u32[]{:S(2)}, u32[]{:S(2)}) collective-permute-start(f32[2,1,512]{2,0,1:T(2,128)S(1)} %get-tuple-element.532), channel_id=1, source_target_pairs={{0,2},{2,4},{4,6},{6,8},{8,10},{10,12},{12,14},{14,16},{16,18},{18... | collective-permute-start | bytes 12296 | tf_op jit(solution)/shard_map/ppermute | solution.py:24
  184.4 13.8 %collective-permute-start.7 = (f32[2,1,16,1024]{3,2,1,0:T(8,128)S(1)}, f32[2,1,16,1024]{3,2,1,0:T(8,128)S(1)}, u32[]{:S(2)}, u32[]{:S(2)}) collective-permute-start(f32[2,1,16,1024]{3,2,1,0:T(8,128)S(1)} %get-tuple-element.519), channel_id=1, source_target_pairs={{0,32},{32,64},{64,96},{96,128},{128,160},{160,192},{192,224},{1,3... | collective-permute-start | bytes 393224 | tf_op jit(solution)/shard_map/ppermute | solution.py:24
  189.7 8.9 %collective-permute-start.6 = (f32[2,1,16,1024]{3,2,1,0:T(8,128)S(1)}, f32[2,1,16,1024]{3,2,1,0:T(8,128)S(1)}, u32[]{:S(2)}, u32[]{:S(2)}) collective-permute-start(f32[2,1,16,1024]{3,2,1,0:T(8,128)S(1)} %get-tuple-element.520), channel_id=1, source_target_pairs={{32,0},{64,32},{96,64},{128,96},{160,128},{192,160},{224,192},{33,... | collective-permute-start | bytes 393224 | tf_op jit(solution)/shard_map/ppermute | solution.py:25
  191.6 17.2 %collective-permute-start.17 = (f32[2,1,512]{2,0,1:T(2,128)S(1)}, f32[2,1,512]{2,0,1:T(2,128)S(1)}, u32[]{:S(2)}, u32[]{:S(2)}) collective-permute-start(f32[2,1,512]{2,0,1:T(2,128)S(1)} %get-tuple-element.533), channel_id=1, source_target_pairs={{2,0},{4,2},{6,4},{8,6},{10,8},{12,10},{14,12},{16,14},{18,16},{20... | collective-permute-start | bytes 12296 | tf_op jit(solution)/shard_map/ppermute | solution.py:25
  200.5 11.0 %collective-permute-start.8 = (f32[2,18,1,1024]{3,1,2,0:T(8,128)S(1)}, f32[2,18,1,1024]{3,1,2,0:T(8,128)S(1)}, u32[]{:S(2)}, u32[]{:S(2)}) collective-permute-start(f32[2,18,1,1024]{3,1,2,0:T(8,128)S(1)} %copy.95), channel_id=1, source_target_pairs={{2,0},{4,2},{6,4},{8,6},{10,8},{12,10},{14,12},{16,14},{18,16},{20... | collective-permute-start | bytes 442376 | tf_op jit(solution)/shard_map/ppermute | solution.py:25
  206.9 10.9 %collective-permute-start.9 = (f32[2,18,1,1024]{3,1,2,0:T(8,128)S(1)}, f32[2,18,1,1024]{3,1,2,0:T(8,128)S(1)}, u32[]{:S(2)}, u32[]{:S(2)}) collective-permute-start(f32[2,18,1,1024]{3,1,2,0:T(8,128)S(1)} %copy.97), channel_id=1, source_target_pairs={{0,2},{2,4},{4,6},{6,8},{8,10},{10,12},{12,14},{14,16},{16,18},{18... | collective-permute-start | bytes 442376 | tf_op jit(solution)/shard_map/ppermute | solution.py:24
  219.2 18.6 %collective-permute-start.10 = (f32[2,18,18,1]{3,2,1,0:T(8,128)}, f32[2,18,18,1]{3,2,1,0:T(8,128)}, u32[]{:S(2)}, u32[]{:S(2)}) collective-permute-start(f32[2,18,18,1]{3,2,1,0:T(8,128)} %get-tuple-element.499), channel_id=1, source_target_pairs={{1,0},{3,2},{5,4},{7,6},{9,8},{11,10},{13,12},{15,14},{17,16},{19,... | collective-permute-start | bytes 7784 | tf_op jit(solution)/shard_map/ppermute | solution.py:25
  220.6 17.2 %collective-permute-start.11 = (f32[2,18,18,1]{3,2,1,0:T(8,128)}, f32[2,18,18,1]{3,2,1,0:T(8,128)}, u32[]{:S(2)}, u32[]{:S(2)}) collective-permute-start(f32[2,18,18,1]{3,2,1,0:T(8,128)} %get-tuple-element.500), channel_id=1, source_target_pairs={{0,1},{2,3},{4,5},{6,7},{8,9},{10,11},{12,13},{14,15},{16,17},{18,... | collective-permute-start | bytes 7784 | tf_op jit(solution)/shard_map/ppermute | solution.py:24
  270.5 61.7 %copy-start.38 = (f32[96,32]{1,0:T(8,128)S(1)}, f32[96,32]{1,0:T(8,128)}, u32[]{:S(2)}) copy-start(f32[96,32]{1,0:T(8,128)} %copy.138) | copy-start | bytes 36868
  270.5 63.8 %copy-start.70 = (s32[2048]{0:T(1024)S(1)}, s32[2048]{0:T(1024)}, u32[]{:S(2)}) copy-start(s32[2048]{0:T(1024)} %copy-done.69) | copy-start | bytes 24580
  316.0 94.5 %collective-permute-start.19 = (f32[2,1,16,1024]{3,2,1,0:T(8,128)}, f32[2,1,16,1024]{3,2,1,0:T(8,128)}, u32[]{:S(2)}, u32[]{:S(2)}) collective-permute-start(f32[2,1,16,1024]{3,2,1,0:T(8,128)} %get-tuple-element.517), channel_id=1, source_target_pairs={{0,32},{32,64},{64,96},{96,128},{128,160},{160,192},{192,224},{1,3... | collective-permute-start | bytes 393224 | tf_op jit(solution)/shard_map/ppermute | solution.py:24
  318.0 92.5 %collective-permute-start.18 = (f32[2,1,16,1024]{3,2,1,0:T(8,128)}, f32[2,1,16,1024]{3,2,1,0:T(8,128)}, u32[]{:S(2)}, u32[]{:S(2)}) collective-permute-start(f32[2,1,16,1024]{3,2,1,0:T(8,128)} %get-tuple-element.518), channel_id=1, source_target_pairs={{32,0},{64,32},{96,64},{128,96},{160,128},{192,160},{224,192},{33,... | collective-permute-start | bytes 393224 | tf_op jit(solution)/shard_map/ppermute | solution.py:25
  343.8 61.3 %copy-start.32 = (f32[128,32]{1,0:T(8,128)S(1)}, f32[128,32]{1,0:T(8,128)}, u32[]{:S(2)}) copy-start(f32[128,32]{1,0:T(8,128)} %scatter-add.209) | copy-start | bytes 49156
  343.8 63.6 %copy-start.36 = (f32[96,32]{1,0:T(8,128)S(1)}, f32[96,32]{1,0:T(8,128)}, u32[]{:S(2)}) copy-start(f32[96,32]{1,0:T(8,128)} %scatter-add.206) | copy-start | bytes 36868
  344.5 10.1 %collective-permute-start.24 = (f32[2,1,512]{2,0,1:T(2,128)S(1)}, f32[2,1,512]{2,0,1:T(2,128)S(1)}, u32[]{:S(2)}, u32[]{:S(2)}) collective-permute-start(f32[2,1,512]{2,0,1:T(2,128)S(1)} %get-tuple-element.530), channel_id=1, source_target_pairs={{0,2},{2,4},{4,6},{6,8},{8,10},{10,12},{12,14},{14,16},{16,18},{18... | collective-permute-start | bytes 12296 | tf_op jit(solution)/shard_map/ppermute | solution.py:24
  348.6 7.3 collective-permute-start.25
  412.5 9.5 %collective-permute-start.20 = (f32[2,18,1,1024]{3,1,2,0:T(8,128)S(1)}, f32[2,18,1,1024]{3,1,2,0:T(8,128)S(1)}, u32[]{:S(2)}, u32[]{:S(2)}) collective-permute-start(f32[2,18,1,1024]{3,1,2,0:T(8,128)S(1)} %copy.109), channel_id=1, source_target_pairs={{2,0},{4,2},{6,4},{8,6},{10,8},{12,10},{14,12},{16,14},{18,16},{20... | collective-permute-start | bytes 442376 | tf_op jit(solution)/shard_map/ppermute | solution.py:25
  418.8 9.7 %collective-permute-start.21 = (f32[2,18,1,1024]{3,1,2,0:T(8,128)S(1)}, f32[2,18,1,1024]{3,1,2,0:T(8,128)S(1)}, u32[]{:S(2)}, u32[]{:S(2)}) collective-permute-start(f32[2,18,1,1024]{3,1,2,0:T(8,128)S(1)} %copy.111), channel_id=1, source_target_pairs={{0,2},{2,4},{4,6},{6,8},{8,10},{10,12},{12,14},{14,16},{16,18},{18... | collective-permute-start | bytes 442376 | tf_op jit(solution)/shard_map/ppermute | solution.py:24
  430.6 36.8 %collective-permute-start.22 = (f32[2,18,18,1]{3,2,1,0:T(8,128)}, f32[2,18,18,1]{3,2,1,0:T(8,128)}, u32[]{:S(2)}, u32[]{:S(2)}) collective-permute-start(f32[2,18,18,1]{3,2,1,0:T(8,128)} %get-tuple-element.497), channel_id=1, source_target_pairs={{1,0},{3,2},{5,4},{7,6},{9,8},{11,10},{13,12},{15,14},{17,16},{19,... | collective-permute-start | bytes 7784 | tf_op jit(solution)/shard_map/ppermute | solution.py:25
  431.9 35.5 %collective-permute-start.23 = (f32[2,18,18,1]{3,2,1,0:T(8,128)}, f32[2,18,18,1]{3,2,1,0:T(8,128)}, u32[]{:S(2)}, u32[]{:S(2)}) collective-permute-start(f32[2,18,18,1]{3,2,1,0:T(8,128)} %get-tuple-element.498), channel_id=1, source_target_pairs={{0,1},{2,3},{4,5},{6,7},{8,9},{10,11},{12,13},{14,15},{16,17},{18,... | collective-permute-start | bytes 7784 | tf_op jit(solution)/shard_map/ppermute | solution.py:24
  501.3 16.2 %collective-permute-start.32 = (f32[2,1,512]{2,0,1:T(2,128)S(1)}, f32[2,1,512]{2,0,1:T(2,128)S(1)}, u32[]{:S(2)}, u32[]{:S(2)}) collective-permute-start(f32[2,1,512]{2,0,1:T(2,128)S(1)} %get-tuple-element.528), channel_id=1, source_target_pairs={{0,2},{2,4},{4,6},{6,8},{8,10},{10,12},{12,14},{14,16},{16,18},{18... | collective-permute-start | bytes 12296 | tf_op jit(solution)/shard_map/ppermute | solution.py:24
  505.6 12.6 %collective-permute-start.27 = (f32[2,1,16,1024]{3,2,1,0:T(8,128)S(1)}, f32[2,1,16,1024]{3,2,1,0:T(8,128)S(1)}, u32[]{:S(2)}, u32[]{:S(2)}) collective-permute-start(f32[2,1,16,1024]{3,2,1,0:T(8,128)S(1)} %get-tuple-element.515), channel_id=1, source_target_pairs={{0,32},{32,64},{64,96},{96,128},{128,160},{160,192},{192,224},{1,3... | collective-permute-start | bytes 393224 | tf_op jit(solution)/shard_map/ppermute | solution.py:24
  508.8 9.4 %collective-permute-start.26 = (f32[2,1,16,1024]{3,2,1,0:T(8,128)S(1)}, f32[2,1,16,1024]{3,2,1,0:T(8,128)S(1)}, u32[]{:S(2)}, u32[]{:S(2)}) collective-permute-start(f32[2,1,16,1024]{3,2,1,0:T(8,128)S(1)} %get-tuple-element.516), channel_id=1, source_target_pairs={{32,0},{64,32},{96,64},{128,96},{160,128},{192,160},{224,192},{33,... | collective-permute-start | bytes 393224 | tf_op jit(solution)/shard_map/ppermute | solution.py:25
  511.5 15.3 %collective-permute-start.33 = (f32[2,1,512]{2,0,1:T(2,128)S(1)}, f32[2,1,512]{2,0,1:T(2,128)S(1)}, u32[]{:S(2)}, u32[]{:S(2)}) collective-permute-start(f32[2,1,512]{2,0,1:T(2,128)S(1)} %get-tuple-element.529), channel_id=1, source_target_pairs={{2,0},{4,2},{6,4},{8,6},{10,8},{12,10},{14,12},{16,14},{18,16},{20... | collective-permute-start | bytes 12296 | tf_op jit(solution)/shard_map/ppermute | solution.py:25
  520.2 7.9 %collective-permute-start.28 = (f32[2,18,1,1024]{3,1,2,0:T(8,128)S(1)}, f32[2,18,1,1024]{3,1,2,0:T(8,128)S(1)}, u32[]{:S(2)}, u32[]{:S(2)}) collective-permute-start(f32[2,18,1,1024]{3,1,2,0:T(8,128)S(1)} %copy.115), channel_id=1, source_target_pairs={{2,0},{4,2},{6,4},{8,6},{10,8},{12,10},{14,12},{16,14},{18,16},{20... | collective-permute-start | bytes 442376 | tf_op jit(solution)/shard_map/ppermute | solution.py:25
  524.9 9.7 %collective-permute-start.29 = (f32[2,18,1,1024]{3,1,2,0:T(8,128)S(1)}, f32[2,18,1,1024]{3,1,2,0:T(8,128)S(1)}, u32[]{:S(2)}, u32[]{:S(2)}) collective-permute-start(f32[2,18,1,1024]{3,1,2,0:T(8,128)S(1)} %copy.117), channel_id=1, source_target_pairs={{0,2},{2,4},{4,6},{6,8},{8,10},{10,12},{12,14},{14,16},{16,18},{18... | collective-permute-start | bytes 442376 | tf_op jit(solution)/shard_map/ppermute | solution.py:24
  536.0 21.6 %collective-permute-start.30 = (f32[2,18,18,1]{3,2,1,0:T(8,128)}, f32[2,18,18,1]{3,2,1,0:T(8,128)}, u32[]{:S(2)}, u32[]{:S(2)}) collective-permute-start(f32[2,18,18,1]{3,2,1,0:T(8,128)} %get-tuple-element.495), channel_id=1, source_target_pairs={{1,0},{3,2},{5,4},{7,6},{9,8},{11,10},{13,12},{15,14},{17,16},{19,... | collective-permute-start | bytes 7784 | tf_op jit(solution)/shard_map/ppermute | solution.py:25
  537.4 20.1 %collective-permute-start.31 = (f32[2,18,18,1]{3,2,1,0:T(8,128)}, f32[2,18,18,1]{3,2,1,0:T(8,128)}, u32[]{:S(2)}, u32[]{:S(2)}) collective-permute-start(f32[2,18,18,1]{3,2,1,0:T(8,128)} %get-tuple-element.496), channel_id=1, source_target_pairs={{0,1},{2,3},{4,5},{6,7},{8,9},{10,11},{12,13},{14,15},{16,17},{18,... | collective-permute-start | bytes 7784 | tf_op jit(solution)/shard_map/ppermute | solution.py:24
  645.6 38.9 %collective-permute-start.35 = (f32[2,1,16,1024]{3,2,1,0:T(8,128)}, f32[2,1,16,1024]{3,2,1,0:T(8,128)S(1)}, u32[]{:S(2)}, u32[]{:S(2)}) collective-permute-start(f32[2,1,16,1024]{3,2,1,0:T(8,128)} %get-tuple-element.513), channel_id=1, source_target_pairs={{0,32},{32,64},{64,96},{96,128},{128,160},{160,192},{192,224},{1,3... | collective-permute-start | bytes 393224 | tf_op jit(solution)/shard_map/ppermute | solution.py:24
  647.5 37.0 %collective-permute-start.34 = (f32[2,1,16,1024]{3,2,1,0:T(8,128)}, f32[2,1,16,1024]{3,2,1,0:T(8,128)S(1)}, u32[]{:S(2)}, u32[]{:S(2)}) collective-permute-start(f32[2,1,16,1024]{3,2,1,0:T(8,128)} %get-tuple-element.514), channel_id=1, source_target_pairs={{32,0},{64,32},{96,64},{128,96},{160,128},{192,160},{224,192},{33,... | collective-permute-start | bytes 393224 | tf_op jit(solution)/shard_map/ppermute | solution.py:25
  660.8 8.9 %collective-permute-start.40 = (f32[2,1,512]{2,0,1:T(2,128)S(1)}, f32[2,1,512]{2,0,1:T(2,128)S(1)}, u32[]{:S(2)}, u32[]{:S(2)}) collective-permute-start(f32[2,1,512]{2,0,1:T(2,128)S(1)} %get-tuple-element.526), channel_id=1, source_target_pairs={{0,2},{2,4},{4,6},{6,8},{8,10},{10,12},{12,14},{14,16},{16,18},{18... | collective-permute-start | bytes 12296 | tf_op jit(solution)/shard_map/ppermute | solution.py:24
  663.7 7.3 collective-permute-start.41
  686.5 9.5 %collective-permute-start.36 = (f32[2,18,1,1024]{3,1,2,0:T(8,128)S(1)}, f32[2,18,1,1024]{3,1,2,0:T(8,128)S(1)}, u32[]{:S(2)}, u32[]{:S(2)}) collective-permute-start(f32[2,18,1,1024]{3,1,2,0:T(8,128)S(1)} %copy.121), channel_id=1, source_target_pairs={{2,0},{4,2},{6,4},{8,6},{10,8},{12,10},{14,12},{16,14},{18,16},{20... | collective-permute-start | bytes 442376 | tf_op jit(solution)/shard_map/ppermute | solution.py:25
  692.8 9.7 %collective-permute-start.37 = (f32[2,18,1,1024]{3,1,2,0:T(8,128)S(1)}, f32[2,18,1,1024]{3,1,2,0:T(8,128)S(1)}, u32[]{:S(2)}, u32[]{:S(2)}) collective-permute-start(f32[2,18,1,1024]{3,1,2,0:T(8,128)S(1)} %copy.123), channel_id=1, source_target_pairs={{0,2},{2,4},{4,6},{6,8},{8,10},{10,12},{12,14},{14,16},{16,18},{18... | collective-permute-start | bytes 442376 | tf_op jit(solution)/shard_map/ppermute | solution.py:24
  703.9 46.3 %collective-permute-start.38 = (f32[2,18,18,1]{3,2,1,0:T(8,128)}, f32[2,18,18,1]{3,2,1,0:T(8,128)}, u32[]{:S(2)}, u32[]{:S(2)}) collective-permute-start(f32[2,18,18,1]{3,2,1,0:T(8,128)} %get-tuple-element.493), channel_id=1, source_target_pairs={{1,0},{3,2},{5,4},{7,6},{9,8},{11,10},{13,12},{15,14},{17,16},{19,... | collective-permute-start | bytes 7784 | tf_op jit(solution)/shard_map/ppermute | solution.py:25
  705.3 44.9 %collective-permute-start.39 = (f32[2,18,18,1]{3,2,1,0:T(8,128)}, f32[2,18,18,1]{3,2,1,0:T(8,128)}, u32[]{:S(2)}, u32[]{:S(2)}) collective-permute-start(f32[2,18,18,1]{3,2,1,0:T(8,128)} %get-tuple-element.494), channel_id=1, source_target_pairs={{0,1},{2,3},{4,5},{6,7},{8,9},{10,11},{12,13},{14,15},{16,17},{18,... | collective-permute-start | bytes 7784 | tf_op jit(solution)/shard_map/ppermute | solution.py:24
  (122 other events, 2596.9 us)
where the time goes:
time: 786 us; the launch traced here: 771 us
  other arithmetic  381 us (48%)
  local copies, waits for them, and re-layouts  207 us (26%)
  starting transfers between devices  144 us (18%)
  waiting for transfers between devices  35.3 us (4%)
    ppermute x21, starting transfers between devices, extended(): after = lax.ppermute(leading, axis, down)  81.7 us
    div x4, other arithmetic, shards(): new_x = (adjoint_rhs + near_sum + coupling * back[None]) / diag_x  77.8 us
    ppermute x21, starting transfers between devices, extended(): before = lax.ppermute(last, axis, up)  62.7 us
    scatter-add x5, other arithmetic, shards(): jnp.zeros((per_row,), jnp.float32).at[arrived_flat]  57 us
    gather x12, local copies, waits for them, and re-layouts, shards(): picked = weight * mixed[voxel_index]  50.4 us
    add x32, other arithmetic, particle_update(): numer = rhs_block + rate[None, :] * inner  46 us
    div x32, other arithmetic, particle_update(): scaled = block / volume[:, None]  41.5 us
    gather x4, local copies, waits for them, and re-layouts, shards(): answers = last[arrived_slot]  41.3 us
  transfers between devices with their start and end apart: 42, of which 12 were waited for; matrix products, arithmetic and copies ran while one was open for 43% of the time, Pallas kernels for 0%

commit v1 on v0

v1 whole, which is shorter than its diff:
```python
import jax
import jax.numpy as jnp
from jax import lax
from jax.experimental import pallas as pl
from jax.experimental.pallas import tpu as pltpu
from jax.sharding import PartitionSpec as P

ITERS = 4
shell_counts = (64, 80, 96, 128, 160, 192, 224, 256)
shell_starts = tuple(sum(shell_counts[:i]) for i in range(8))
conduct = ((1.0, 0.1, 0.5), (1.0, 0.05, 0.3))
masses = ((1.0, 0.5, 0.8), (1.0, 2.0, 1.5))
coupling = (1.0, 0.5)
groups = ((0, 128), (128, 256))
PACKED = 384

F32 = jnp.float32
BF16 = jnp.bfloat16
MESH = pl.DeviceIdType.MESH
N = 16


def pick(phase, values):
    return jnp.where(phase == 0, values[0], jnp.where(phase == 1, values[1], values[2]))


def inverse(d):
    r = pl.reciprocal(d, approx=True)
    r = r * (2.0 - d * r)
    return r * (2.0 - d * r)


def face(a, b):
    return 2.0 * a * b * inverse(a + b)


def split(v):
    hi = v.astype(BF16)
    lo = (v - hi.astype(F32)).astype(BF16)
    return hi, lo


def ahead(x, row, lane, sub):
    t = jnp.where(lane == 0, pltpu.roll(x, 7, 0), x)
    t = jnp.where((lane == 0) & (sub == 7), row, t)
    return pltpu.roll(t, 127, 1)


def behind(x, row, lane, sub):
    t = jnp.where(lane == 127, pltpu.roll(x, 1, 0), x)
    t = jnp.where((lane == 127) & (sub == 0), row, t)
    return pltpu.roll(t, 1, 1)


def dot(a, b):
    return jnp.dot(a, b, preferred_element_type=F32)


def dot_t(a, b):
    return lax.dot_general(a, b, (((1,), (1,)), ((), ())), preferred_element_type=F32)


def kernel(
    rhs_h, cond_h, phase_h, prhs_h, rate_ref, gamma_ref, vox_ref, slot_ref, wgt_ref,
    xo_h, yo_ref,
    rhs, cond, phase, prhs,
    kap, fx, fy, fzp, fzm, inv, xb, hx, hy, hz, cx, cy,
    back, m1, m0, m2, r1, r0, r2, r1t, r0t, r2t, sel, wc, q_scr, vc, rec, rect,
    yb, ydn, yup, yrhs, gsurf, lsend, lrecv, ssend, srecv,
    in_sem, out_sem, send_sem, recv_sem,
):
    gx = lax.axis_index("gx")
    gy = lax.axis_index("gy")
    gz = lax.axis_index("gz")
    nx, ny = lax.axis_size("gx"), lax.axis_size("gy")
    x_dn = {"gx": lax.rem(gx + nx - 1, nx)}
    x_up = {"gx": lax.rem(gx + 1, nx)}
    y_dn = {"gy": lax.rem(gy + ny - 1, ny)}
    y_up = {"gy": lax.rem(gy + 1, ny)}
    z_other = {"gz": 1 - gz}
    z_row = 7 * (1 - gz)

    copies = [
        pltpu.make_async_copy(src, dst, in_sem.at[n])
        for n, (src, dst) in enumerate(
            ((cond_h, cond), (phase_h, phase), (rhs_h, rhs), (prhs_h, prhs))
        )
    ]
    for copy in copies:
        copy.start()

    lsend[...] = jnp.zeros((8, 128), F32)
    ssend[...] = jnp.zeros((2, 8, 128), F32)
    barrier = pltpu.get_barrier_semaphore()
    for peer in (x_dn, x_up, y_dn, y_up, z_other):
        pl.semaphore_signal(barrier, inc=1, device_id=peer, device_id_type=MESH)
    pl.semaphore_wait(barrier, 5)

    def remote(src, dst, e, n, peer):
        return pltpu.make_async_remote_copy(
            src_ref=src, dst_ref=dst, send_sem=send_sem.at[e, n], recv_sem=recv_sem.at[e, n],
            device_id=peer, device_id_type=MESH,
        )

    def halo_copies(src, e):
        return (
            remote(src.at[:, 0], hx.at[e, 1], e, 0, x_dn),
            remote(src.at[:, N - 1], hx.at[e, 0], e, 1, x_up),
            remote(src.at[:, :, 0], hy.at[e, 1], e, 2, y_dn),
            remote(src.at[:, :, N - 1], hy.at[e, 0], e, 3, y_up),
            remote(src.at[:, :, :, z_row], hz.at[e], e, 4, z_other),
        )

    def sum_copies(e):
        return (
            remote(ssend.at[0], srecv.at[e, 1], e, 5, y_dn),
            remote(ssend.at[1], srecv.at[e, 0], e, 6, y_up),
        )

    def last_copies(e):
        return (
            remote(lsend, lrecv.at[e, 1], e, 7, y_dn),
            remote(lsend, lrecv.at[e, 0], e, 8, y_up),
        )

    lane = lax.broadcasted_iota(jnp.int32, (8, 128), 1)
    sub = lax.broadcasted_iota(jnp.int32, (8, 128), 0)

    copies[0].wait()
    copies[1].wait()

    def kappa_plane(i, _):
        for j in range(N):
            c, p = cond[i, j], phase[i, j]
            for f in range(2):
                kap[f, i, j] = c * pick(p, conduct[f])
        return 0

    lax.fori_loop(0, N, kappa_plane, 0)
    kap_copies = halo_copies(kap, 0)
    for copy in kap_copies:
        copy.start()

    rec[...] = jnp.zeros((128, 128), F32)
    for o in range(3):
        for q in range(4):
            at = pl.ds(128 * q, 128)
            rec[pl.ds(o * 4 + q, 1), :] = vox_ref[pl.ds(o, 1), at].astype(F32)
            rec[pl.ds(12 + o * 4 + q, 1), :] = slot_ref[pl.ds(o, 1), at].astype(F32)
            rec[pl.ds(24 + o * 4 + q, 1), :] = wgt_ref[pl.ds(o, 1), at]
    rect[...] = jnp.transpose(rec[...])

    for o, ref, width in ((0, r0, 512), (1, r1, 2048), (2, r2, 512)):
        for q in range(4):
            n = o * 4 + q
            voxel = rect[:, n : n + 1]
            slot = rect[:, 12 + n : 13 + n]
            weight = rect[:, 24 + n : 25 + n]
            row = jnp.floor(voxel * (1.0 / 128.0))
            at_lane = voxel - row * 128.0
            if o != 1:
                plane = jnp.floor(row * (1.0 / 128.0))
                row = row - plane * 96.0 - (96.0 if o == 2 else 0.0)
            lanes = lax.broadcasted_iota(jnp.int32, (128, 128), 1).astype(F32)
            wc[o, pl.ds(128 * q, 128), :] = jnp.where(lanes == at_lane, weight, 0.0)
            for h in range(2):
                hit = (lanes + 128.0 * h) == slot
                sel[o, pl.ds(128 * q, 128), pl.ds(128 * h, 128)] = jnp.where(hit, 1.0, 0.0).astype(BF16)
            for h in range(width // 128):
                hit = (lanes + 128.0 * h) == row
                ref[pl.ds(128 * q, 128), pl.ds(128 * h, 128)] = jnp.where(hit, 1.0, 0.0).astype(BF16)

    for o, ref, width in ((0, r0t, 512), (1, r1t, 2048), (2, r2t, 512)):
        row = lax.shift_right_logical(vox_ref[pl.ds(o, 1), :], 7)
        if o != 1:
            row = row - lax.shift_right_logical(row, 7) * 96 - (96 if o == 2 else 0)

        def fill(c, _, ref=ref, row=row):
            at = pl.multiple_of(c * 64, 64)
            down = lax.broadcasted_iota(jnp.int32, (64, 512), 0) + at
            ref[pl.ds(at, 64), :] = jnp.where(down == row, 1.0, 0.0).astype(BF16)
            return 0

        lax.fori_loop(0, width // 64, fill, 0)

    def particle_sums(src):
        sums = []
        for o in range(3):
            both = jnp.concatenate(split(src[o]), axis=1)
            per_record = dot_t(jnp.ones((16, 256), BF16), both)
            parts = dot(jnp.concatenate(split(per_record), axis=0), sel[o])
            sums.append(parts[0:1] + parts[16:17])
        return sums

    def send_sums(sums, e):
        for d, s in ((0, sums[0]), (1, sums[2])):
            ssend[d, 0:1, :] = s[:, :128]
            ssend[d, 1:2, :] = s[:, 128:]
        for copy in sum_copies(e):
            copy.start()
        return sums[1]

    def to_voxels():
        full = dot(r1t[...], vc[1])
        back[...] = full[:, :128] + full[:, 128:]
        for o, ref, base in ((0, r0t, 0), (2, r2t, 96)):
            part = dot(ref[...], vc[o])
            part = part[:, :128] + part[:, 128:]
            for i in range(N):
                back[pl.ds(i * 128 + base, 32), :] += part[i * 32 : i * 32 + 32]

    own_weight = send_sums(particle_sums(wc), 0)
    for o in range(3):
        hi, lo = split(wc[o])
        vc[o, :, 0:128] = hi
        vc[o, :, 128:256] = lo
    to_voxels()

    kap_copies[4].wait_recv()
    first_z = (gz == 0).astype(F32)

    fx[:, 0] = jnp.zeros((2, N, 8, 128), F32)
    fx[:, N] = jnp.zeros((2, N, 8, 128), F32)

    def face_plane(i, _):
        below = jnp.maximum(i - 1, 0)
        not_first = (i > 0).astype(F32)
        for f in range(2):
            for j in range(N):
                k = kap[f, i, j]
                row = jnp.broadcast_to(hz[0, f, i, pl.ds(j, 1), :], (8, 128))
                fx[f, i, j] = not_first * face(k, kap[f, below, j])
                if j:
                    fy[f, i, j] = face(k, kap[f, i, j - 1])
                nxt = ahead(k, row * first_z, lane, sub)
                up = face(k, nxt)
                fzp[f, i, j] = up
                prev = behind(k, row * (1.0 - first_z), lane, sub)
                fzm[f, i, j] = face(k, prev)
        return 0

    lax.fori_loop(0, N, face_plane, 0)

    def diag_plane(i, _):
        for f in range(2):
            for j in range(N):
                d = pick(phase[i, j], masses[f]) + coupling[f] * back[pl.ds(pl.multiple_of(i * 128 + j * 8, 8), 8), :]
                d = d + fx[f, i, j] + fx[f, i + 1, j] + fzp[f, i, j] + fzm[f, i, j]
                if j:
                    d = d + fy[f, i, j]
                if j < N - 1:
                    d = d + fy[f, i, j + 1]
                inv[f, i, j] = d
        return 0

    lax.fori_loop(0, N, diag_plane, 0)

    for copy in kap_copies[:4]:
        copy.wait_recv()
    inside = (
        (gx > 0).astype(F32), (gx < nx - 1).astype(F32),
        (gy > 0).astype(F32), (gy < ny - 1).astype(F32),
    )

    def rim_faces(n, _):
        for f in range(2):
            for d, at in ((0, 0), (1, N - 1)):
                c = inside[d] * face(kap[f, at, n], hx[0, d, f, n])
                cx[d, f, n] = c
                inv[f, at, n] += c
            for d, at in ((0, 0), (1, N - 1)):
                c = inside[2 + d] * face(kap[f, n, at], hy[0, d, f, n])
                cy[d, f, n] = c
                inv[f, n, at] += c
        return 0

    lax.fori_loop(0, N, rim_faces, 0)
    copies[2].wait()

    def start_plane(i, _):
        for f in range(2):
            for j in range(N):
                v = inverse(inv[f, i, j])
                inv[f, i, j] = v
                xb[0, f, i, j] = rhs[f, i, j] * v
        return 0

    lax.fori_loop(0, N, start_plane, 0)

    def rim_scale(n, _):
        for f in range(2):
            for d, at in ((0, 0), (1, N - 1)):
                cx[d, f, n] *= inv[f, at, n]
                cy[d, f, n] *= inv[f, n, at]
        return 0

    lax.fori_loop(0, N, rim_scale, 0)

    copies[3].wait()
    yb[0] = jnp.zeros((PACKED, 128), F32)
    rates = []
    for g, (base, rows) in enumerate(groups):
        for c in range(4):
            cls = 4 * g + c
            count = shell_counts[cls]
            yb[0, pl.ds(base + rows - count, count), 32 * c : 32 * c + 32] = prhs[
                pl.ds(shell_starts[cls], count), :
            ]
        rates.append(
            [
                jnp.concatenate([ref[4 * g + c : 4 * g + c + 1, :] for c in range(4)], axis=1)
                for ref in (rate_ref, gamma_ref)
            ]
        )
    for copy in sum_copies(0):
        copy.wait_recv()
    for g, (base, rows) in enumerate(groups):
        rate, gamma = rates[g]
        sums = own_weight[:, 128 * g : 128 * g + 128] + srecv[0, 0, g : g + 1, :] + srecv[0, 1, g : g + 1, :]
        down = lax.broadcasted_iota(jnp.int32, (rows, 128), 0)
        part = lax.broadcasted_iota(jnp.int32, (rows, 128), 1) // 32
        cnt = shell_counts[4 * g : 4 * g + 4]
        count = jnp.where(part == 0, cnt[0], jnp.where(part == 1, cnt[1], jnp.where(part == 2, cnt[2], cnt[3])))
        s = (down - (rows - count)).astype(F32)
        live = s >= 0.0
        last = down == rows - 1
        count = count.astype(F32)
        unit = inverse(count)
        lower = jnp.where(live, (s * unit) * (s * unit), 0.0)
        upper = jnp.where(live & ~last, ((s + 1.0) * unit) * ((s + 1.0) * unit), 0.0)
        cube = 3.0 * count * count

        def over_volume(s):
            return cube * inverse(3.0 * s * s + 3.0 * s + 1.0)

        d = 1.0 + rate * ((upper + lower) * over_volume(s))
        d = d + jnp.where(last, gamma * (coupling[0] + coupling[1]) * sums, 0.0)
        d = inverse(d)
        at = pl.ds(base, rows)
        ydn[at, :] = rate * lower * over_volume(s - 1.0) * d
        yup[at, :] = rate * upper * over_volume(s + 1.0) * d
        y = yb[0, at, :] * d
        yrhs[at, :] = y
        yb[0, at, :] = y
        gsurf[pl.ds(g, 1), :] = gamma * d[rows - 1 : rows]

    for copy in kap_copies + sum_copies(0):
        copy.wait_send()

    def iteration(t, _):
        e = t + 1
        cur = lax.rem(t, 2)
        new = 1 - cur
        x = xb.at[cur]
        xn = xb.at[new]
        halos = halo_copies(x, e)
        for copy in halos:
            copy.start()
        own_last = jnp.concatenate([yb[0, 127:128, :], yb[0, 383:384, :]], axis=1)
        lsend[0:1, :] = yb[0, 127:128, :]
        lsend[1:2, :] = yb[0, 383:384, :]
        lasts = last_copies(e)
        for copy in lasts:
            copy.start()

        def mix(i, _):
            for jp in range(N // 2):
                at = pl.ds(2 * jp, 2)
                v = coupling[0] * x[0, i, at] + coupling[1] * x[1, i, at]
                hi, lo = split(v.reshape(16, 128))
                targets = [(m1, i * 128 + jp * 16)]
                if jp < 2:
                    targets.append((m0, i * 32 + jp * 16))
                if jp >= 6:
                    targets.append((m2, i * 32 + (jp - 6) * 16))
                for ref, start in targets:
                    rows = pl.ds(pl.multiple_of(start, 16), 16)
                    ref[rows, 0:128] = hi
                    ref[rows, 128:256] = lo
            return 0

        lax.fori_loop(0, N, mix, 0)
        for o, ref, m in ((0, r0, m0), (2, r2, m2), (1, r1, m1)):
            got = dot(ref[...], m[...])
            q_scr[o] = (got[:, :128] + got[:, 128:]) * wc[o]
        own_sum = send_sums(particle_sums(q_scr), e)

        for copy in lasts:
            copy.wait_recv()
        for o in range(3):
            if o == 1:
                table = own_last
            else:
                table = jnp.concatenate([lrecv[e, o // 2, 0:1, :], lrecv[e, o // 2, 1:2, :]], axis=1)
            hi, lo = split(table)
            table = jnp.concatenate(
                [jnp.broadcast_to(hi, (128, 256)), jnp.broadcast_to(lo, (128, 256))], axis=0
            )
            got = dot_t(sel[o], table)
            hi, lo = split((got[:, :128] + got[:, 128:]) * wc[o])
            vc[o, :, 0:128] = hi
            vc[o, :, 128:256] = lo
        to_voxels()

        halos[4].wait_recv()

        def plane(i, _):
            below = jnp.maximum(i - 1, 0)
            above = jnp.minimum(i + 1, N - 1)
            for j in range(N):
                b = back[pl.ds(pl.multiple_of(i * 128 + j * 8, 8), 8), :]
                for f in range(2):
                    v = x[f, i, j]
                    row = jnp.broadcast_to(hz[e, f, i, pl.ds(j, 1), :], (8, 128))
                    acc = rhs[f, i, j] + coupling[f] * b
                    acc += fx[f, i, j] * x[f, below, j]
                    acc += fx[f, i + 1, j] * x[f, above, j]
                    if j:
                        acc += fy[f, i, j] * x[f, i, j - 1]
                    if j < N - 1:
                        acc += fy[f, i, j + 1] * x[f, i, j + 1]
                    acc += fzp[f, i, j] * ahead(v, row, lane, sub)
                    acc += fzm[f, i, j] * behind(v, row, lane, sub)
                    xn[f, i, j] = acc * inv[f, i, j]
            return 0

        lax.fori_loop(0, N, plane, 0)

        for copy in sum_copies(e):
            copy.wait_recv()
        y = yb[0]
        y = yrhs[...] + ydn[...] * pltpu.roll(y, 1, 0) + yup[...] * pltpu.roll(y, PACKED - 1, 0)
        yb[0] = y
        for g, row in ((0, 127), (1, 383)):
            sums = own_sum[:, 128 * g : 128 * g + 128] + srecv[e, 0, g : g + 1, :] + srecv[e, 1, g : g + 1, :]
            yb[0, row : row + 1, :] += gsurf[pl.ds(g, 1), :] * sums

        for copy in halos[:4]:
            copy.wait_recv()

        def rim(n, _):
            for f in range(2):
                for d, at in ((0, 0), (1, N - 1)):
                    xn[f, at, n] += cx[d, f, n] * hx[e, d, f, n]
                for d, at in ((0, 0), (1, N - 1)):
                    xn[f, n, at] += cy[d, f, n] * hy[e, d, f, n]
            return 0

        lax.fori_loop(0, N, rim, 0)
        for copy in halos + lasts + sum_copies(e):
            copy.wait_send()
        return 0

    lax.fori_loop(0, ITERS, iteration, 0)

    out = pltpu.make_async_copy(xb.at[0], xo_h, out_sem)
    out.start()
    for g, (base, rows) in enumerate(groups):
        for c in range(4):
            cls = 4 * g + c
            count = shell_counts[cls]
            yo_ref[pl.ds(shell_starts[cls], count), :] = yb[
                0, pl.ds(base + rows - count, count), 32 * c : 32 * c + 32
            ]
    out.wait()


def shards(
    adjoint_rhs, conductance, phase, particle_rhs, diffusion_rate, exchange_rate,
    record_voxel, record_slot, record_weight,
):
    vmem = pl.BlockSpec(memory_space=pltpu.VMEM)
    hbm = pl.BlockSpec(memory_space=pl.ANY)
    field = (2, N, N, 8, 128)
    col = (8, 128)
    scratch = [
        pltpu.VMEM(field, F32),
        pltpu.VMEM(field[1:], F32),
        pltpu.VMEM(field[1:], jnp.int32),
        pltpu.VMEM((1200, 32), F32),
        pltpu.VMEM(field, F32),
        pltpu.VMEM((2, N + 1, N, *col), F32),
        pltpu.VMEM(field, F32),
        pltpu.VMEM(field, F32),
        pltpu.VMEM(field, F32),
        pltpu.VMEM(field, F32),
        pltpu.VMEM((2, *field), F32),
        pltpu.VMEM((5, 2, 2, N, *col), F32),
        pltpu.VMEM((5, 2, 2, N, *col), F32),
        pltpu.VMEM((5, 2, N, N, 128), F32),
        pltpu.VMEM((2, 2, N, *col), F32),
        pltpu.VMEM((2, 2, N, *col), F32),
        pltpu.VMEM((2048, 128), F32),
        pltpu.VMEM((2048, 256), BF16),
        pltpu.VMEM((512, 256), BF16),
        pltpu.VMEM((512, 256), BF16),
        pltpu.VMEM((512, 2048), BF16),
        pltpu.VMEM((512, 512), BF16),
        pltpu.VMEM((512, 512), BF16),
        pltpu.VMEM((2048, 512), BF16),
        pltpu.VMEM((512, 512), BF16),
        pltpu.VMEM((512, 512), BF16),
        pltpu.VMEM((3, 512, 256), BF16),
        pltpu.VMEM((3, 512, 128), F32),
        pltpu.VMEM((3, 512, 128), F32),
        pltpu.VMEM((3, 512, 256), BF16),
        pltpu.VMEM((128, 128), F32),
        pltpu.VMEM((128, 128), F32),
        pltpu.VMEM((1, PACKED, 128), F32),
        pltpu.VMEM((PACKED, 128), F32),
        pltpu.VMEM((PACKED, 128), F32),
        pltpu.VMEM((PACKED, 128), F32),
        pltpu.VMEM(col, F32),
        pltpu.VMEM(col, F32),
        pltpu.VMEM((5, 2, *col), F32),
        pltpu.VMEM((2, *col), F32),
        pltpu.VMEM((5, 2, *col), F32),
        pltpu.SemaphoreType.DMA((4,)),
        pltpu.SemaphoreType.DMA,
        pltpu.SemaphoreType.DMA((5, 9)),
        pltpu.SemaphoreType.DMA((5, 9)),
    ]
    x, y = pl.pallas_call(
        kernel,
        out_shape=(
            jax.ShapeDtypeStruct(field, F32),
            jax.ShapeDtypeStruct((1200, 32), F32),
        ),
        in_specs=[hbm, hbm, hbm, hbm, vmem, vmem, vmem, vmem, vmem],
        out_specs=(hbm, vmem),
        scratch_shapes=scratch,
        compiler_params=pltpu.CompilerParams(
            collective_id=0, has_side_effects=True, vmem_limit_bytes=56 * 1024 * 1024
        ),
    )(
        adjoint_rhs.reshape(field),
        conductance.reshape(field[1:]),
        phase.reshape(field[1:]),
        particle_rhs,
        diffusion_rate,
        exchange_rate,
        record_voxel.reshape(3, 512),
        record_slot.reshape(3, 512),
        record_weight.reshape(3, 512),
    )
    return x.reshape(2, N, N, 1024), y


def solution(mesh):
    grid = P("gx", "gy", "gz")
    parts = P(None, ("gx", "gy", "gz"))
    return jax.shard_map(
        shards,
        mesh=mesh,
        in_specs=(P(None, "gx", "gy", "gz"), grid, grid, parts, parts, parts, grid, grid, grid),
        out_specs=(P(None, "gx", "gy", "gz"), parts),
        check_vma=False,
    )
```

time: 786 us -> 220 us (0.28)
  the two profiles are of different devices: /device:TPU:104 before, /device:TPU:2 now
where the time goes in v1:
time: 220 us
  Pallas kernels  205 us (93%)
  local copies, waits for them, and re-layouts  13.8 us (6%)
    pallas_call x1, Pallas kernels, shards(): pl.pallas_call(kernel, out_shape=(jax.ShapeDtypeStruct(field, F32), jax.S...  205 us
    unnamed x13, local copies, waits for them, and re-layouts  11.1 us

profile of v1, /device:TPU:2, one launch (start us, length us, event | category | flops | bytes accessed | tf_op | source)
XLA Modules:
  0.0 219.6 jit_solution(2505559161778252629)
XLA Ops:
  0.6 0.0 copy-start.1
  0.6 1.4 copy.22
  2.0 1.3 copy_bitcast_fusion.1
  3.3 2.0 copy.11.prhs_h
  5.3 0.0 copy-start
  5.3 2.6 %copy.17 = f32[32,8,8,128]{3,2,1,0:T(8,128)} copy(f32[32,8,8,128]{3,1,2,0:T(8,128)} %bitcast.26) | data formatting | bytes 2097152
  7.9 0.0 copy-done.1
  7.9 1.2 copy.18
  9.1 0.0 copy-done
  9.1 1.8 copy.16
  10.8 205.1 %shard_map.104 = (f32[2,16,16,8,128]{4,3,2,1,0:T(8,128)}, f32[1200,32]{1,0:T(8,128)}) custom-call(f32[2,16,16,8,128]{4,3,2,1,0:T(8,128)} %bitcast.22, f32[16,16,8,128]{3,2,1,0:T(8,128)} %bitcast.23, s32[16,16,8,128]{3,2,1,0:T(8,128)} %bitcast.24, f32[1200,32]{1,0:T(8,128)} %copy.11.prhs_h, f32[8,32]{1,0:T(8,128)} %rate_ref.1, f32[8,32]{1,0:T(8,128)} %gamma_ref.1, ...), custom_call_target="tpu_custom_call" | custom-call | tf_op jit(solution)/shard_map/pallas_call | solution.py:523
  216.0 0.0 copy-start.2
  216.0 2.8 %reshape.31 = f32[2,16,16,1024]{3,2,1,0:T(8,128)} reshape(f32[2,16,16,8,128]{4,3,2,1,0:T(8,128)} %get-tuple-element.4) | data formatting | bytes 4194304 | tf_op jit(solution)/shard_map/reshape | solution.py:546
  218.8 0.0 copy-done.2
  218.8 0.9 copy.12
Async XLA Ops:
  0.6 7.2 %copy-start.1 = (s32[16,16,1024]{2,1,0:T(8,128)S(1)}, s32[16,16,1024]{2,1,0:T(8,128)}, u32[]{:S(2)}) copy-start(s32[16,16,1024]{2,1,0:T(8,128)} %param.11) | copy-start | bytes 3145732
  5.3 3.7 %copy-start = (f32[2,16,16,1024]{3,2,1,0:T(8,128)S(1)}, f32[2,16,16,1024]{3,2,1,0:T(8,128)}, u32[]{:S(2)}) copy-start(f32[2,16,16,1024]{3,2,1,0:T(8,128)} %param.9) | copy-start | bytes 6291460
  216.0 2.8 %copy-start.2 = (f32[1200,32]{1,0:T(8,128)S(1)}, f32[1200,32]{1,0:T(8,128)}, u32[]{:S(2)}) copy-start(f32[1200,32]{1,0:T(8,128)} %get-tuple-element.7) | copy-start | bytes 460804

commit v2 on v1

--- a/solution.py
+++ b/solution.py
@@ -61,9 +61,9 @@
 
 
 def kernel(
-    rhs_h, cond_h, phase_h, prhs_h, rate_ref, gamma_ref, vox_ref, slot_ref, wgt_ref,
+    rhs_h, cond_h, phase_h, prhs_ref, rate_ref, gamma_ref, vox_ref, slot_ref, wgt_ref,
     xo_h, yo_ref,
-    rhs, cond, phase, prhs,
+    rhs, cond, phase, pack,
     kap, fx, fy, fzp, fzm, inv, xb, hx, hy, hz, cx, cy,
     back, m1, m0, m2, r1, r0, r2, r1t, r0t, r2t, sel, wc, q_scr, vc, rec, rect,
     yb, ydn, yup, yrhs, gsurf, lsend, lrecv, ssend, srecv,
@@ -80,14 +80,20 @@
     z_other = {"gz": 1 - gz}
     z_row = 7 * (1 - gz)
 
-    copies = [
-        pltpu.make_async_copy(src, dst, in_sem.at[n])
-        for n, (src, dst) in enumerate(
-            ((cond_h, cond), (phase_h, phase), (rhs_h, rhs), (prhs_h, prhs))
-        )
+    def tiles(n, z):
+        at = pl.ds(128 * z, 128)
+        return (
+            (cond_h.at[:, :, at], cond.at[:, :, z]),
+            (phase_h.at[:, :, at], phase.at[:, :, z]),
+            (rhs_h.at[:, :, :, at], rhs.at[:, :, :, z]),
+        )[n]
+
+    loads = [
+        [pltpu.make_async_copy(*tiles(n, z), in_sem.at[n, z]) for z in range(8)] for n in range(3)
     ]
-    for copy in copies:
-        copy.start()
+    for load in loads:
+        for copy in load:
+            copy.start()
 
     lsend[...] = jnp.zeros((8, 128), F32)
     ssend[...] = jnp.zeros((2, 8, 128), F32)
@@ -126,8 +132,8 @@
     lane = lax.broadcasted_iota(jnp.int32, (8, 128), 1)
     sub = lax.broadcasted_iota(jnp.int32, (8, 128), 0)
 
-    copies[0].wait()
-    copies[1].wait()
+    for copy in loads[0] + loads[1]:
+        copy.wait()
 
     def kappa_plane(i, _):
         for j in range(N):
@@ -145,9 +151,9 @@
     for o in range(3):
         for q in range(4):
             at = pl.ds(128 * q, 128)
-            rec[pl.ds(o * 4 + q, 1), :] = vox_ref[pl.ds(o, 1), at].astype(F32)
-            rec[pl.ds(12 + o * 4 + q, 1), :] = slot_ref[pl.ds(o, 1), at].astype(F32)
-            rec[pl.ds(24 + o * 4 + q, 1), :] = wgt_ref[pl.ds(o, 1), at]
+            rec[pl.ds(o * 4 + q, 1), :] = vox_ref[o, :, at].astype(F32)
+            rec[pl.ds(12 + o * 4 + q, 1), :] = slot_ref[o, :, at].astype(F32)
+            rec[pl.ds(24 + o * 4 + q, 1), :] = wgt_ref[o, :, at]
     rect[...] = jnp.transpose(rec[...])
 
     for o, ref, width in ((0, r0, 512), (1, r1, 2048), (2, r2, 512)):
@@ -171,7 +177,7 @@
                 ref[pl.ds(128 * q, 128), pl.ds(128 * h, 128)] = jnp.where(hit, 1.0, 0.0).astype(BF16)
 
     for o, ref, width in ((0, r0t, 512), (1, r1t, 2048), (2, r2t, 512)):
-        row = lax.shift_right_logical(vox_ref[pl.ds(o, 1), :], 7)
+        row = lax.shift_right_logical(vox_ref[o], 7)
         if o != 1:
             row = row - lax.shift_right_logical(row, 7) * 96 - (96 if o == 2 else 0)
 
@@ -275,7 +281,8 @@
         return 0
 
     lax.fori_loop(0, N, rim_faces, 0)
-    copies[2].wait()
+    for copy in loads[2]:
+        copy.wait()
 
     def start_plane(i, _):
         for f in range(2):
@@ -296,22 +303,22 @@
 
     lax.fori_loop(0, N, rim_scale, 0)
 
-    copies[3].wait()
-    yb[0] = jnp.zeros((PACKED, 128), F32)
+    pack[...] = jnp.zeros((128, PACKED), F32)
     rates = []
     for g, (base, rows) in enumerate(groups):
         for c in range(4):
             cls = 4 * g + c
             count = shell_counts[cls]
-            yb[0, pl.ds(base + rows - count, count), 32 * c : 32 * c + 32] = prhs[
-                pl.ds(shell_starts[cls], count), :
-            ]
+            start, end = shell_starts[cls], base + rows
+            pack[32 * c : 32 * c + 32, end - count : end] = prhs_ref[:, start : start + count]
         rates.append(
             [
                 jnp.concatenate([ref[4 * g + c : 4 * g + c + 1, :] for c in range(4)], axis=1)
                 for ref in (rate_ref, gamma_ref)
             ]
         )
+    for b in range(0, PACKED, 128):
+        yb[b : b + 128, :] = jnp.transpose(pack[:, b : b + 128])
     for copy in sum_copies(0):
         copy.wait_recv()
     for g, (base, rows) in enumerate(groups):
@@ -339,9 +346,9 @@
         at = pl.ds(base, rows)
         ydn[at, :] = rate * lower * over_volume(s - 1.0) * d
         yup[at, :] = rate * upper * over_volume(s + 1.0) * d
-        y = yb[0, at, :] * d
+        y = yb[at, :] * d
         yrhs[at, :] = y
-        yb[0, at, :] = y
+        yb[at, :] = y
         gsurf[pl.ds(g, 1), :] = gamma * d[rows - 1 : rows]
 
     for copy in kap_copies + sum_copies(0):
@@ -356,9 +363,9 @@
         halos = halo_copies(x, e)
         for copy in halos:
             copy.start()
-        own_last = jnp.concatenate([yb[0, 127:128, :], yb[0, 383:384, :]], axis=1)
-        lsend[0:1, :] = yb[0, 127:128, :]
-        lsend[1:2, :] = yb[0, 383:384, :]
+        own_last = jnp.concatenate([yb[127:128, :], yb[383:384, :]], axis=1)
+        lsend[0:1, :] = yb[127:128, :]
+        lsend[1:2, :] = yb[383:384, :]
         lasts = last_copies(e)
         for copy in lasts:
             copy.start()
@@ -407,6 +414,7 @@
         def plane(i, _):
             below = jnp.maximum(i - 1, 0)
             above = jnp.minimum(i + 1, N - 1)
+            done = []
             for j in range(N):
                 b = back[pl.ds(pl.multiple_of(i * 128 + j * 8, 8), 8), :]
                 for f in range(2):
@@ -421,48 +429,54 @@
                         acc += fy[f, i, j + 1] * x[f, i, j + 1]
                     acc += fzp[f, i, j] * ahead(v, row, lane, sub)
                     acc += fzm[f, i, j] * behind(v, row, lane, sub)
-                    xn[f, i, j] = acc * inv[f, i, j]
+                    done.append((f, j, acc * inv[f, i, j]))
+            for f, j, v in done:
+                xn[f, i, j] = v
             return 0
 
         lax.fori_loop(0, N, plane, 0)
 
         for copy in sum_copies(e):
             copy.wait_recv()
-        y = yb[0]
+        y = yb[...]
         y = yrhs[...] + ydn[...] * pltpu.roll(y, 1, 0) + yup[...] * pltpu.roll(y, PACKED - 1, 0)
-        yb[0] = y
+        yb[...] = y
         for g, row in ((0, 127), (1, 383)):
             sums = own_sum[:, 128 * g : 128 * g + 128] + srecv[e, 0, g : g + 1, :] + srecv[e, 1, g : g + 1, :]
-            yb[0, row : row + 1, :] += gsurf[pl.ds(g, 1), :] * sums
+            yb[row : row + 1, :] += gsurf[pl.ds(g, 1), :] * sums
 
         for copy in halos[:4]:
             copy.wait_recv()
 
-        def rim(n, _):
-            for f in range(2):
-                for d, at in ((0, 0), (1, N - 1)):
-                    xn[f, at, n] += cx[d, f, n] * hx[e, d, f, n]
-                for d, at in ((0, 0), (1, N - 1)):
-                    xn[f, n, at] += cy[d, f, n] * hy[e, d, f, n]
-            return 0
-
-        lax.fori_loop(0, N, rim, 0)
+        for f in range(2):
+            for d, at in ((0, 0), (1, N - 1)):
+                xn[f, at] += cx[d, f] * hx[e, d, f]
+            for d, at in ((0, 0), (1, N - 1)):
+                xn[f, :, at] += cy[d, f] * hy[e, d, f]
         for copy in halos + lasts + sum_copies(e):
             copy.wait_send()
         return 0
 
     lax.fori_loop(0, ITERS, iteration, 0)
 
-    out = pltpu.make_async_copy(xb.at[0], xo_h, out_sem)
-    out.start()
+    outs = [
+        pltpu.make_async_copy(
+            xb.at[0, :, :, :, z], xo_h.at[:, :, :, pl.ds(128 * z, 128)], out_sem.at[z]
+        )
+        for z in range(8)
+    ]
+    for copy in outs:
+        copy.start()
+    for b in range(0, PACKED, 128):
+        pack[:, b : b + 128] = jnp.transpose(yb[b : b + 128, :])
     for g, (base, rows) in enumerate(groups):
         for c in range(4):
             cls = 4 * g + c
             count = shell_counts[cls]
-            yo_ref[pl.ds(shell_starts[cls], count), :] = yb[
-                0, pl.ds(base + rows - count, count), 32 * c : 32 * c + 32
-            ]
-    out.wait()
+            start, end = shell_starts[cls], base + rows
+            yo_ref[:, start : start + count] = pack[32 * c : 32 * c + 32, end - count : end]
+    for copy in outs:
+        copy.wait()
 
 
 def shards(
@@ -477,7 +491,7 @@
         pltpu.VMEM(field, F32),
         pltpu.VMEM(field[1:], F32),
         pltpu.VMEM(field[1:], jnp.int32),
-        pltpu.VMEM((1200, 32), F32),
+        pltpu.VMEM((128, PACKED), F32),
         pltpu.VMEM(field, F32),
         pltpu.VMEM((2, N + 1, N, *col), F32),
         pltpu.VMEM(field, F32),
@@ -506,7 +520,7 @@
         pltpu.VMEM((3, 512, 256), BF16),
         pltpu.VMEM((128, 128), F32),
         pltpu.VMEM((128, 128), F32),
-        pltpu.VMEM((1, PACKED, 128), F32),
+        pltpu.VMEM((PACKED, 128), F32),
         pltpu.VMEM((PACKED, 128), F32),
         pltpu.VMEM((PACKED, 128), F32),
         pltpu.VMEM((PACKED, 128), F32),
@@ -515,35 +529,35 @@
         pltpu.VMEM((5, 2, *col), F32),
         pltpu.VMEM((2, *col), F32),
         pltpu.VMEM((5, 2, *col), F32),
-        pltpu.SemaphoreType.DMA((4,)),
-        pltpu.SemaphoreType.DMA,
+        pltpu.SemaphoreType.DMA((3, 8)),
+        pltpu.SemaphoreType.DMA((8,)),
         pltpu.SemaphoreType.DMA((5, 9)),
         pltpu.SemaphoreType.DMA((5, 9)),
     ]
     x, y = pl.pallas_call(
         kernel,
         out_shape=(
-            jax.ShapeDtypeStruct(field, F32),
-            jax.ShapeDtypeStruct((1200, 32), F32),
+            jax.ShapeDtypeStruct(adjoint_rhs.shape, F32),
+            jax.ShapeDtypeStruct((32, 1200), F32),
         ),
-        in_specs=[hbm, hbm, hbm, hbm, vmem, vmem, vmem, vmem, vmem],
+        in_specs=[hbm, hbm, hbm, vmem, vmem, vmem, vmem, vmem, vmem],
         out_specs=(hbm, vmem),
         scratch_shapes=scratch,
         compiler_params=pltpu.CompilerParams(
             collective_id=0, has_side_effects=True, vmem_limit_bytes=56 * 1024 * 1024
         ),
     )(
-        adjoint_rhs.reshape(field),
-        conductance.reshape(field[1:]),
-        phase.reshape(field[1:]),
-        particle_rhs,
+        adjoint_rhs,
+        conductance,
+        phase,
+        particle_rhs.T,
         diffusion_rate,
         exchange_rate,
-        record_voxel.reshape(3, 512),
-        record_slot.reshape(3, 512),
-        record_weight.reshape(3, 512),
+        record_voxel.reshape(3, 1, 512),
+        record_slot.reshape(3, 1, 512),
+        record_weight.reshape(3, 1, 512),
     )
-    return x.reshape(2, N, N, 1024), y
+    return x, y.T
 
 
 def solution(mesh):

time: 220 us -> 64.8 us (0.29)
  Pallas kernels: 205 us -> 60.2 us
  local copies, waits for them, and re-layouts: 13.8 us -> 3.87 us
    pallas_call x1, Pallas kernels: 205 us -> 60.2 us  [shards(): pl.pallas_call(kernel, out_shape=(jax.ShapeDtypeStruct(adjoint_rhs.shape,...]
    unnamed x13 -> x4, local copies, waits for them, and re-layouts: 11.1 us -> 3.87 us
    reshape x1 -> x0, local copies, waits for them, and re-layouts: 2.77 us -> none  [shards(): return (x.reshape(2, N, N, 1024), y)]
where the time goes in v2:
time: 64.8 us; the launch traced here: 64.7 us
  Pallas kernels  60.2 us (93%)
  local copies, waits for them, and re-layouts  3.87 us (6%)
  between operations  0.65 us (1%)
    pallas_call x1, Pallas kernels, shards(): pl.pallas_call(kernel, out_shape=(jax.ShapeDtypeStruct(adjoint_rhs.shape,...  60.2 us
    unnamed x4, local copies, waits for them, and re-layouts  3.87 us

profile of v2, /device:TPU:2, one launch (start us, length us, event | category | flops | bytes accessed | tf_op | source)
XLA Modules:
  0.0 64.7 jit_solution(16569402820070979819)
XLA Ops:
  0.6 60.2 %shard_map.104 = (f32[2,16,16,1024]{3,2,1,0:T(8,128)}, f32[32,1200]{1,0:T(8,128)}) custom-call(f32[2,16,16,1024]{3,2,1,0:T(8,128)} %rhs_h.1, f32[16,16,1024]{2,1,0:T(8,128)} %cond_h.1, s32[16,16,1024]{2,1,0:T(8,128)} %phase_h.1, f32[32,1200]{1,0:T(8,128)} %bitcast.5, f32[8,32]{1,0:T(8,128)} %rate_ref.1, f32[8,32]{1,0:T(8,128)} %gamma_ref.1, ...), custom_call_target="tpu_custom_call" | custom-call | tf_op jit(solution)/shard_map/pallas_call | solution.py:537
  60.8 0.0 copy-start
  60.8 3.2 %copy.13 = f32[2,16,16,1024]{3,2,1,0:T(8,128)} copy(f32[2,16,16,1024]{3,2,1,0:T(8,128)} %get-tuple-element.8) | data formatting | bytes 4194304
  64.0 0.0 copy-done
  64.0 0.7 %copy.14 = f32[1200,32]{0,1:T(8,128)} copy(f32[1200,32]{0,1:T(8,128)S(1)} %bitcast.6) | data formatting | bytes 307200
Async XLA Ops:
  60.8 3.2 %copy-start = (f32[32,1200]{1,0:T(8,128)S(1)}, f32[32,1200]{1,0:T(8,128)}, u32[]{:S(2)}) copy-start(f32[32,1200]{1,0:T(8,128)} %get-tuple-element.5) | copy-start | bytes 460804

commit v3 on v2

--- a/solution.py
+++ b/solution.py
@@ -25,13 +25,11 @@
 
 
 def inverse(d):
-    r = pl.reciprocal(d, approx=True)
-    r = r * (2.0 - d * r)
-    return r * (2.0 - d * r)
+    return pl.reciprocal(d, approx=True)
 
 
 def face(a, b):
-    return 2.0 * a * b * inverse(a + b)
+    return inverse(a + b)
 
 
 def split(v):
@@ -61,13 +59,13 @@
 
 
 def kernel(
-    rhs_h, cond_h, phase_h, prhs_ref, rate_ref, gamma_ref, vox_ref, slot_ref, wgt_ref,
+    rhs_h, cond_h, phase_h, prhs_h, rate_h, gamma_h, vox_h, slot_h, wgt_h,
     xo_h, yo_ref,
-    rhs, cond, phase, pack,
-    kap, fx, fy, fzp, fzm, inv, xb, hx, hy, hz, cx, cy,
-    back, m1, m0, m2, r1, r0, r2, r1t, r0t, r2t, sel, wc, q_scr, vc, rec, rect,
+    rhs, cond, phase, prhs_ref, rate_ref, gamma_ref, vox_ref, slot_ref, wgt_ref, pack,
+    kap, fx, fy, fzp, fzm, inv, xa, xb, yface, hx, hy, hz, cx, cy,
+    back, got_scr, m0, m2, r1, r0, r2, r1t, r0t, r2t, sel, wc, q_scr, vc, zface, rec, rect,
     yb, ydn, yup, yrhs, gsurf, lsend, lrecv, ssend, srecv,
-    in_sem, out_sem, send_sem, recv_sem,
+    in_sem, small_sem, out_sem, send_sem, recv_sem,
 ):
     gx = lax.axis_index("gx")
     gy = lax.axis_index("gy")
@@ -91,7 +89,16 @@
     loads = [
         [pltpu.make_async_copy(*tiles(n, z), in_sem.at[n, z]) for z in range(8)] for n in range(3)
     ]
-    for load in loads:
+    small = [
+        pltpu.make_async_copy(src, dst, small_sem.at[n])
+        for n, (src, dst) in enumerate(
+            (
+                (vox_h, vox_ref), (slot_h, slot_ref), (wgt_h, wgt_ref),
+                (prhs_h, prhs_ref), (rate_h, rate_ref), (gamma_h, gamma_ref),
+            )
+        )
+    ]
+    for load in [small] + loads:
         for copy in load:
             copy.start()
 
@@ -100,7 +107,6 @@
     barrier = pltpu.get_barrier_semaphore()
     for peer in (x_dn, x_up, y_dn, y_up, z_other):
         pl.semaphore_signal(barrier, inc=1, device_id=peer, device_id_type=MESH)
-    pl.semaphore_wait(barrier, 5)
 
     def remote(src, dst, e, n, peer):
         return pltpu.make_async_remote_copy(
@@ -112,10 +118,18 @@
         return (
             remote(src.at[:, 0], hx.at[e, 1], e, 0, x_dn),
             remote(src.at[:, N - 1], hx.at[e, 0], e, 1, x_up),
-            remote(src.at[:, :, 0], hy.at[e, 1], e, 2, y_dn),
-            remote(src.at[:, :, N - 1], hy.at[e, 0], e, 3, y_up),
+            remote(yface.at[0], hy.at[e, 1], e, 2, y_dn),
+            remote(yface.at[1], hy.at[e, 0], e, 3, y_up),
             remote(src.at[:, :, :, z_row], hz.at[e], e, 4, z_other),
         )
+
+    def start_halos(src, e):
+        yface[0] = src[:, :, 0]
+        yface[1] = src[:, :, N - 1]
+        started = halo_copies(src, e)
+        for copy in started:
+            copy.start()
+        return started
 
     def sum_copies(e):
         return (
@@ -129,23 +143,17 @@
             remote(lsend, lrecv.at[e, 0], e, 8, y_up),
         )
 
+    def start_lasts(e):
+        lsend[0:1, :] = yb[127:128, :]
+        lsend[1:2, :] = yb[383:384, :]
+        for copy in last_copies(e):
+            copy.start()
+
     lane = lax.broadcasted_iota(jnp.int32, (8, 128), 1)
     sub = lax.broadcasted_iota(jnp.int32, (8, 128), 0)
 
-    for copy in loads[0] + loads[1]:
+    for copy in small:
         copy.wait()
-
-    def kappa_plane(i, _):
-        for j in range(N):
-            c, p = cond[i, j], phase[i, j]
-            for f in range(2):
-                kap[f, i, j] = c * pick(p, conduct[f])
-        return 0
-
-    lax.fori_loop(0, N, kappa_plane, 0)
-    kap_copies = halo_copies(kap, 0)
-    for copy in kap_copies:
-        copy.start()
 
     rec[...] = jnp.zeros((128, 128), F32)
     for o in range(3):
@@ -215,51 +223,68 @@
             for i in range(N):
                 back[pl.ds(i * 128 + base, 32), :] += part[i * 32 : i * 32 + 32]
 
-    own_weight = send_sums(particle_sums(wc), 0)
     for o in range(3):
         hi, lo = split(wc[o])
         vc[o, :, 0:128] = hi
         vc[o, :, 128:256] = lo
     to_voxels()
 
+    for copy in loads[0] + loads[1]:
+        copy.wait()
+
+    def kappa_plane(i, _):
+        for j in range(N):
+            c, p = cond[i, j], phase[i, j]
+            r = inverse(c)
+            for f in range(2):
+                kap[f, i, j] = r * pick(p, [0.5 / v for v in conduct[f]])
+        return 0
+
+    lax.fori_loop(0, N, kappa_plane, 0)
+    pl.semaphore_wait(barrier, 5)
+    kap_copies = start_halos(kap, 0)
+    own_weight = send_sums(particle_sums(wc), 0)
+
     kap_copies[4].wait_recv()
     first_z = (gz == 0).astype(F32)
+    end_mask = jnp.where((lane == 127) & (sub == 7), first_z, 1.0)
 
     fx[:, 0] = jnp.zeros((2, N, 8, 128), F32)
-    fx[:, N] = jnp.zeros((2, N, 8, 128), F32)
+    for f in range(2):
+        for i in range(N):
+            start = face(kap[f, i, :, 0, :], pltpu.roll(hz[0, f, i], 1, 1))
+            zface[f, i] = pltpu.roll(start, 127, 1) * (1.0 - first_z)
 
     def face_plane(i, _):
         below = jnp.maximum(i - 1, 0)
+        above = jnp.minimum(i + 1, N - 1)
         not_first = (i > 0).astype(F32)
-        for f in range(2):
-            for j in range(N):
+        not_last = (i < N - 1).astype(F32)
+        for j in range(N):
+            p = phase[i, j]
+            weight = back[pl.ds(pl.multiple_of(i * 128 + j * 8, 8), 8), :]
+            for f in range(2):
+                row = jnp.broadcast_to(hz[0, f, i, pl.ds(j, 1), :], (8, 128))
+                start = jnp.broadcast_to(zface[f, i, pl.ds(j, 1), :], (8, 128))
                 k = kap[f, i, j]
-                row = jnp.broadcast_to(hz[0, f, i, pl.ds(j, 1), :], (8, 128))
-                fx[f, i, j] = not_first * face(k, kap[f, below, j])
+                d = pick(p, masses[f]) + coupling[f] * weight
+                upper = not_last * face(k, kap[f, above, j])
+                fx[f, i + 1, j] = upper
+                d += upper + not_first * face(k, kap[f, below, j])
                 if j:
-                    fy[f, i, j] = face(k, kap[f, i, j - 1])
-                nxt = ahead(k, row * first_z, lane, sub)
-                up = face(k, nxt)
+                    d += face(k, kap[f, i, j - 1])
+                if j < N - 1:
+                    side = face(k, kap[f, i, j + 1])
+                    fy[f, i, j + 1] = side
+                    d += side
+                up = face(k, ahead(k, row, lane, sub)) * end_mask
+                down = behind(up, start, lane, sub)
                 fzp[f, i, j] = up
-                prev = behind(k, row * (1.0 - first_z), lane, sub)
-                fzm[f, i, j] = face(k, prev)
+                fzm[f, i, j] = down
+                inv[f, i, j] = d + up + down
         return 0
 
     lax.fori_loop(0, N, face_plane, 0)
-
-    def diag_plane(i, _):
-        for f in range(2):
-            for j in range(N):
-                d = pick(phase[i, j], masses[f]) + coupling[f] * back[pl.ds(pl.multiple_of(i * 128 + j * 8, 8), 8), :]
-                d = d + fx[f, i, j] + fx[f, i + 1, j] + fzp[f, i, j] + fzm[f, i, j]
-                if j:
-                    d = d + fy[f, i, j]
-                if j < N - 1:
-                    d = d + fy[f, i, j + 1]
-                inv[f, i, j] = d
-        return 0
-
-    lax.fori_loop(0, N, diag_plane, 0)
 
     for copy in kap_copies[:4]:
         copy.wait_recv()
@@ -289,10 +314,13 @@
             for j in range(N):
                 v = inverse(inv[f, i, j])
                 inv[f, i, j] = v
-                xb[0, f, i, j] = rhs[f, i, j] * v
+                xa[f, i, j] = rhs[f, i, j] * v
         return 0
 
     lax.fori_loop(0, N, start_plane, 0)
+    for copy in kap_copies:
+        copy.wait_send()
+    start_halos(xa, 1)
 
     def rim_scale(n, _):
         for f in range(2):
@@ -351,44 +379,57 @@
         yb[at, :] = y
         gsurf[pl.ds(g, 1), :] = gamma * d[rows - 1 : rows]
 
-    for copy in kap_copies + sum_copies(0):
+    for copy in sum_copies(0):
         copy.wait_send()
-
-    def iteration(t, _):
+    start_lasts(1)
+
+    def iteration(t, x, xn):
         e = t + 1
-        cur = lax.rem(t, 2)
-        new = 1 - cur
-        x = xb.at[cur]
-        xn = xb.at[new]
+        own_last = jnp.concatenate([yb[127:128, :], yb[383:384, :]], axis=1)
+        lasts = last_copies(e)
         halos = halo_copies(x, e)
-        for copy in halos:
-            copy.start()
-        own_last = jnp.concatenate([yb[127:128, :], yb[383:384, :]], axis=1)
-        lsend[0:1, :] = yb[127:128, :]
-        lsend[1:2, :] = yb[383:384, :]
-        lasts = last_copies(e)
-        for copy in lasts:
-            copy.start()
-
-        def mix(i, _):
-            for jp in range(N // 2):
-                at = pl.ds(2 * jp, 2)
-                v = coupling[0] * x[0, i, at] + coupling[1] * x[1, i, at]
-                hi, lo = split(v.reshape(16, 128))
-                targets = [(m1, i * 128 + jp * 16)]
-                if jp < 2:
-                    targets.append((m0, i * 32 + jp * 16))
-                if jp >= 6:
-                    targets.append((m2, i * 32 + (jp - 6) * 16))
-                for ref, start in targets:
-                    rows = pl.ds(pl.multiple_of(start, 16), 16)
-                    ref[rows, 0:128] = hi
-                    ref[rows, 128:256] = lo
+
+        got_scr[...] = jnp.zeros((512, 256), F32)
+        halos[4].wait_recv()
+
+        def planes(s, _):
+            mixed = []
+            for h in range(2):
+                i = 2 * s + h
+                below = jnp.maximum(i - 1, 0)
+                above = jnp.minimum(i + 1, N - 1)
+                for j in range(N):
+                    mixed.append(coupling[0] * x[0, i, j] + coupling[1] * x[1, i, j])
+                    for f in range(2):
+                        v = x[f, i, j]
+                        row = jnp.broadcast_to(hz[e, f, i, pl.ds(j, 1), :], (8, 128))
+                        acc = rhs[f, i, j]
+                        acc += fx[f, i, j] * x[f, below, j]
+                        acc += fx[f, i + 1, j] * x[f, above, j]
+                        if j:
+                            acc += fy[f, i, j] * x[f, i, j - 1]
+                        if j < N - 1:
+                            acc += fy[f, i, j + 1] * x[f, i, j + 1]
+                        acc += fzp[f, i, j] * ahead(v, row, lane, sub)
+                        acc += fzm[f, i, j] * behind(v, row, lane, sub)
+                        xn[f, i, j] = acc * inv[f, i, j]
+            parts = []
+            for n in range(0, 2 * N, 2):
+                h, j = divmod(n, N)
+                part = jnp.concatenate(split(jnp.concatenate(mixed[n : n + 2], axis=0)), axis=1)
+                parts.append(part)
+                for ref, first in ((m0, 0), (m2, 12)):
+                    if first <= j < first + 4:
+                        at = (2 * s + h) * 32 + (j - first) * 8
+                        ref[pl.ds(pl.multiple_of(at, 16), 16), :] = part
+            at = pl.ds(pl.multiple_of(s * 256, 256), 256)
+            got_scr[...] += dot(r1[:, at], jnp.concatenate(parts, axis=0))
             return 0
 
-        lax.fori_loop(0, N, mix, 0)
-        for o, ref, m in ((0, r0, m0), (2, r2, m2), (1, r1, m1)):
-            got = dot(ref[...], m[...])
+        lax.fori_loop(0, N // 2, planes, 0)
+
+        for o, ref, m in ((0, r0, m0), (2, r2, m2), (1, None, None)):
+            got = got_scr[...] if o == 1 else dot(ref[...], m[...])
             q_scr[o] = (got[:, :128] + got[:, 128:]) * wc[o]
         own_sum = send_sums(particle_sums(q_scr), e)
 
@@ -409,32 +450,28 @@
             vc[o, :, 128:256] = lo
         to_voxels()
 
-        halos[4].wait_recv()
-
-        def plane(i, _):
-            below = jnp.maximum(i - 1, 0)
-            above = jnp.minimum(i + 1, N - 1)
-            done = []
-            for j in range(N):
-                b = back[pl.ds(pl.multiple_of(i * 128 + j * 8, 8), 8), :]
-                for f in range(2):
-                    v = x[f, i, j]
-                    row = jnp.broadcast_to(hz[e, f, i, pl.ds(j, 1), :], (8, 128))
-                    acc = rhs[f, i, j] + coupling[f] * b
-                    acc += fx[f, i, j] * x[f, below, j]
-                    acc += fx[f, i + 1, j] * x[f, above, j]
-                    if j:
-                        acc += fy[f, i, j] * x[f, i, j - 1]
-                    if j < N - 1:
-                        acc += fy[f, i, j + 1] * x[f, i, j + 1]
-                    acc += fzp[f, i, j] * ahead(v, row, lane, sub)
-                    acc += fzm[f, i, j] * behind(v, row, lane, sub)
-                    done.append((f, j, acc * inv[f, i, j]))
-            for f, j, v in done:
-                xn[f, i, j] = v
+        def records(i, _):
+            rows = pl.ds(pl.multiple_of(i * 128, 128), 128)
+            b = back[rows, :].reshape(N, 8, 128)
+            sums = [xn[f, i] + coupling[f] * b * inv[f, i] for f in range(2)]
+            for f in range(2):
+                xn[f, i] = sums[f]
             return 0
 
-        lax.fori_loop(0, N, plane, 0)
+        lax.fori_loop(0, N, records, 0)
+        for copy in halos[:4]:
+            copy.wait_recv()
+        for f in range(2):
+            for d, at in ((0, 0), (1, N - 1)):
+                xn[f, at] += cx[d, f] * hx[e, d, f]
+            for d, at in ((0, 0), (1, N - 1)):
+                xn[f, :, at] += cy[d, f] * hy[e, d, f]
+        for copy in halos:
+            copy.wait_send()
+
+        @pl.when(t < ITERS - 1)
+        def _():
+            start_halos(xn, e + 1)
 
         for copy in sum_copies(e):
             copy.wait_recv()
@@ -444,24 +481,23 @@
         for g, row in ((0, 127), (1, 383)):
             sums = own_sum[:, 128 * g : 128 * g + 128] + srecv[e, 0, g : g + 1, :] + srecv[e, 1, g : g + 1, :]
             yb[row : row + 1, :] += gsurf[pl.ds(g, 1), :] * sums
-
-        for copy in halos[:4]:
-            copy.wait_recv()
-
-        for f in range(2):
-            for d, at in ((0, 0), (1, N - 1)):
-                xn[f, at] += cx[d, f] * hx[e, d, f]
-            for d, at in ((0, 0), (1, N - 1)):
-                xn[f, :, at] += cy[d, f] * hy[e, d, f]
-        for copy in halos + lasts + sum_copies(e):
+        for copy in lasts + sum_copies(e):
             copy.wait_send()
+
+        @pl.when(t < ITERS - 1)
+        def _():
+            start_lasts(e + 1)
+
+    def two_iterations(u, _):
+        iteration(2 * u, xa, xb)
+        iteration(2 * u + 1, xb, xa)
         return 0
 
-    lax.fori_loop(0, ITERS, iteration, 0)
+    lax.fori_loop(0, ITERS // 2, two_iterations, 0)
 
     outs = [
         pltpu.make_async_copy(
-            xb.at[0, :, :, :, z], xo_h.at[:, :, :, pl.ds(128 * z, 128)], out_sem.at[z]
+            xa.at[:, :, :, z], xo_h.at[:, :, :, pl.ds(128 * z, 128)], out_sem.at[z]
         )
         for z in range(8)
     ]
@@ -484,13 +520,20 @@
     record_voxel, record_slot, record_weight,
 ):
     vmem = pl.BlockSpec(memory_space=pltpu.VMEM)
-    hbm = pl.BlockSpec(memory_space=pl.ANY)
+    hbm = pl.BlockSpec(memory_space=pltpu.HBM)
+    free = pl.BlockSpec(memory_space=pl.ANY)
     field = (2, N, N, 8, 128)
     col = (8, 128)
     scratch = [
         pltpu.VMEM(field, F32),
         pltpu.VMEM(field[1:], F32),
         pltpu.VMEM(field[1:], jnp.int32),
+        pltpu.VMEM((32, 1200), F32),
+        pltpu.VMEM((8, 32), F32),
+        pltpu.VMEM((8, 32), F32),
+        pltpu.VMEM((3, 1, 512), jnp.int32),
+        pltpu.VMEM((3, 1, 512), jnp.int32),
+        pltpu.VMEM((3, 1, 512), F32),
         pltpu.VMEM((128, PACKED), F32),
         pltpu.VMEM(field, F32),
         pltpu.VMEM((2, N + 1, N, *col), F32),
@@ -498,14 +541,16 @@
         pltpu.VMEM(field, F32),
         pltpu.VMEM(field, F32),
         pltpu.VMEM(field, F32),
-        pltpu.VMEM((2, *field), F32),
+        pltpu.VMEM(field, F32),
+        pltpu.VMEM(field, F32),
+        pltpu.VMEM((2, 2, N, *col), F32),
         pltpu.VMEM((5, 2, 2, N, *col), F32),
         pltpu.VMEM((5, 2, 2, N, *col), F32),
         pltpu.VMEM((5, 2, N, N, 128), F32),
         pltpu.VMEM((2, 2, N, *col), F32),
         pltpu.VMEM((2, 2, N, *col), F32),
         pltpu.VMEM((2048, 128), F32),
-        pltpu.VMEM((2048, 256), BF16),
+        pltpu.VMEM((512, 256), F32),
         pltpu.VMEM((512, 256), BF16),
         pltpu.VMEM((512, 256), BF16),
         pltpu.VMEM((512, 2048), BF16),
@@ -518,6 +563,7 @@
         pltpu.VMEM((3, 512, 128), F32),
         pltpu.VMEM((3, 512, 128), F32),
         pltpu.VMEM((3, 512, 256), BF16),
+        pltpu.VMEM((2, N, N, 128), F32),
         pltpu.VMEM((128, 128), F32),
         pltpu.VMEM((128, 128), F32),
         pltpu.VMEM((PACKED, 128), F32),
@@ -530,6 +576,7 @@
         pltpu.VMEM((2, *col), F32),
         pltpu.VMEM((5, 2, *col), F32),
         pltpu.SemaphoreType.DMA((3, 8)),
+        pltpu.SemaphoreType.DMA((6,)),
         pltpu.SemaphoreType.DMA((8,)),
         pltpu.SemaphoreType.DMA((5, 9)),
         pltpu.SemaphoreType.DMA((5, 9)),
@@ -540,8 +587,8 @@
             jax.ShapeDtypeStruct(adjoint_rhs.shape, F32),
             jax.ShapeDtypeStruct((32, 1200), F32),
         ),
-        in_specs=[hbm, hbm, hbm, vmem, vmem, vmem, vmem, vmem, vmem],
-        out_specs=(hbm, vmem),
+        in_specs=[hbm] * 9,
+        out_specs=(free, vmem),
         scratch_shapes=scratch,
         compiler_params=pltpu.CompilerParams(
             collective_id=0, has_side_effects=True, vmem_limit_bytes=56 * 1024 * 1024

time: 64.8 us -> 58.7 us (0.906)
  the two profiles are of different devices: /device:TPU:2 before, /device:TPU:1 now
where the time goes in v3:
time: 58.7 us; the launch traced here: 58.6 us
  Pallas kernels  54.1 us (92%)
  local copies, waits for them, and re-layouts  3.87 us (7%)
  between operations  0.65 us (1%)
    pallas_call x1, Pallas kernels, shards(): pl.pallas_call(kernel, out_shape=(jax.ShapeDtypeStruct(adjoint_rhs.shape,...  54.1 us
    unnamed x4, local copies, waits for them, and re-layouts  3.87 us

profile of v3, /device:TPU:1, one launch (start us, length us, event | category | flops | bytes accessed | tf_op | source)
XLA Modules:
  0.0 58.6 jit_solution(8020383474652303944)
XLA Ops:
  0.6 54.1 %shard_map.104 = (f32[2,16,16,1024]{3,2,1,0:T(8,128)}, f32[32,1200]{1,0:T(8,128)}) custom-call(f32[2,16,16,1024]{3,2,1,0:T(8,128)} %rhs_h.1, f32[16,16,1024]{2,1,0:T(8,128)} %cond_h.1, s32[16,16,1024]{2,1,0:T(8,128)} %phase_h.1, f32[32,1200]{1,0:T(8,128)} %bitcast.5, f32[8,32]{1,0:T(8,128)} %rate_h.1, f32[8,32]{1,0:T(8,128)} %gamma_h.1, ...), custom_call_target="tpu_custom_call" | custom-call | tf_op jit(solution)/shard_map/pallas_call | solution.py:584
  54.7 0.0 copy-start
  54.8 3.2 %copy.13 = f32[2,16,16,1024]{3,2,1,0:T(8,128)} copy(f32[2,16,16,1024]{3,2,1,0:T(8,128)} %get-tuple-element.8) | data formatting | bytes 4194304
  57.9 0.0 copy-done
  58.0 0.7 %copy.14 = f32[1200,32]{0,1:T(8,128)} copy(f32[1200,32]{0,1:T(8,128)S(1)} %bitcast.6) | data formatting | bytes 307200
Async XLA Ops:
  54.7 3.2 %copy-start = (f32[32,1200]{1,0:T(8,128)S(1)}, f32[32,1200]{1,0:T(8,128)}, u32[]{:S(2)}) copy-start(f32[32,1200]{1,0:T(8,128)} %get-tuple-element.5) | copy-start | bytes 460804

commit v4 on v3

--- a/solution.py
+++ b/solution.py
@@ -56,6 +56,20 @@
 
 def dot_t(a, b):
     return lax.dot_general(a, b, (((1,), (1,)), ((), ())), preferred_element_type=F32)
+
+
+class Guarded:
+    def __init__(self, copy, sends, receives):
+        self.copy, self.sends, self.receives = copy, sends, receives
+
+    def start(self):
+        pl.when(self.sends)(self.copy.start)
+
+    def wait_send(self):
+        pl.when(self.sends)(self.copy.wait_send)
+
+    def wait_recv(self):
+        pl.when(self.receives)(self.copy.wait_recv)
 
 
 def kernel(
@@ -102,17 +116,45 @@
         for copy in load:
             copy.start()
 
+    has_x_dn, has_x_up = gx > 0, gx < nx - 1
+    has_y_dn, has_y_up = gy > 0, gy < ny - 1
+    ways = {}
+    for n in (0, 2, 5, 7):
+        dn, up = (has_x_dn, has_x_up) if n == 0 else (has_y_dn, has_y_up)
+        ways[n], ways[n + 1] = (dn, up), (up, dn)
+
+    for missing, ref, d in (
+        (gx == 0, hx, 0), (gx == nx - 1, hx, 1), (gy == 0, hy, 0), (gy == ny - 1, hy, 1)
+    ):
+
+        @pl.when(missing)
+        def _(ref=ref, d=d):
+            ref[:, d] = jnp.zeros((5, 2, N, 8, 128), F32)
+
+    lrecv[...] = jnp.zeros((5, 2, 8, 128), F32)
+    srecv[...] = jnp.zeros((5, 2, 8, 128), F32)
     lsend[...] = jnp.zeros((8, 128), F32)
     ssend[...] = jnp.zeros((2, 8, 128), F32)
     barrier = pltpu.get_barrier_semaphore()
-    for peer in (x_dn, x_up, y_dn, y_up, z_other):
-        pl.semaphore_signal(barrier, inc=1, device_id=peer, device_id_type=MESH)
+    greeted = jnp.int32(1)
+    pl.semaphore_signal(barrier, inc=1, device_id=z_other, device_id_type=MESH)
+    for there, peer in ((has_x_dn, x_dn), (has_x_up, x_up), (has_y_dn, y_dn), (has_y_up, y_up)):
+        greeted += there.astype(jnp.int32)
+
+        @pl.when(there)
+        def _(peer=peer):
+            pl.semaphore_signal(barrier, inc=1, device_id=peer, device_id_type=MESH)
+
 
     def remote(src, dst, e, n, peer):
-        return pltpu.make_async_remote_copy(
+        copy = pltpu.make_async_remote_copy(
             src_ref=src, dst_ref=dst, send_sem=send_sem.at[e, n], recv_sem=recv_sem.at[e, n],
             device_id=peer, device_id_type=MESH,
         )
+        if n == 4:
+            return copy
+        sends, receives = ways[n]
+        return Guarded(copy, sends, receives)
 
     def halo_copies(src, e):
         return (
@@ -241,7 +283,7 @@
         return 0
 
     lax.fori_loop(0, N, kappa_plane, 0)
-    pl.semaphore_wait(barrier, 5)
+    pl.semaphore_wait(barrier, greeted)
     kap_copies = start_halos(kap, 0)
     own_weight = send_sums(particle_sums(wc), 0)
 
@@ -383,6 +425,13 @@
         copy.wait_send()
     start_lasts(1)
 
+    outs = [
+        pltpu.make_async_copy(
+            xa.at[:, :, :, z], xo_h.at[:, :, :, pl.ds(128 * z, 128)], out_sem.at[z]
+        )
+        for z in range(8)
+    ]
+
     def iteration(t, x, xn):
         e = t + 1
         own_last = jnp.concatenate([yb[127:128, :], yb[383:384, :]], axis=1)
@@ -473,6 +522,13 @@
         def _():
             start_halos(xn, e + 1)
 
+        if xn is xa:
+
+            @pl.when(t == ITERS - 1)
+            def _():
+                for copy in outs:
+                    copy.start()
+
         for copy in sum_copies(e):
             copy.wait_recv()
         y = yb[...]
@@ -495,14 +551,6 @@
 
     lax.fori_loop(0, ITERS // 2, two_iterations, 0)
 
-    outs = [
-        pltpu.make_async_copy(
-            xa.at[:, :, :, z], xo_h.at[:, :, :, pl.ds(128 * z, 128)], out_sem.at[z]
-        )
-        for z in range(8)
-    ]
-    for copy in outs:
-        copy.start()
     for b in range(0, PACKED, 128):
         pack[:, b : b + 128] = jnp.transpose(yb[b : b + 128, :])
     for g, (base, rows) in enumerate(groups):
@@ -584,14 +632,14 @@
     x, y = pl.pallas_call(
         kernel,
         out_shape=(
-            jax.ShapeDtypeStruct(adjoint_rhs.shape, F32),
-            jax.ShapeDtypeStruct((32, 1200), F32),
+            pltpu.VMEM(adjoint_rhs.shape, F32),
+            pltpu.VMEM((32, 1200), F32),
         ),
         in_specs=[hbm] * 9,
         out_specs=(free, vmem),
         scratch_shapes=scratch,
         compiler_params=pltpu.CompilerParams(
-            collective_id=0, has_side_effects=True, vmem_limit_bytes=56 * 1024 * 1024
+            collective_id=0, has_side_effects=True, vmem_limit_bytes=52 * 1024 * 1024
         ),
     )(
         adjoint_rhs,

time: 58.7 us -> 48.2 us (0.82)
  the two profiles are of different devices: /device:TPU:1 before, /device:TPU:120 now
where the time goes in v4:
time: 48.2 us; the launch traced here: 48.1 us
  Pallas kernels  45.5 us (94%)
  local copies, waits for them, and re-layouts  1.99 us (4%)
  between operations  0.64 us (1%)
    pallas_call x1, Pallas kernels, shards(): pl.pallas_call(kernel, out_shape=(pltpu.VMEM(adjoint_rhs.shape, F32), plt...  45.5 us
    unnamed x2, local copies, waits for them, and re-layouts  1.99 us

profile of v4, /device:TPU:120, one launch (start us, length us, event | category | flops | bytes accessed | tf_op | source)
XLA Modules:
  0.0 48.1 jit_solution(7611771936408532212)
XLA Ops:
  0.6 45.5 %shard_map.104 = (f32[2,16,16,1024]{3,2,1,0:T(8,128)S(1)}, f32[32,1200]{1,0:T(8,128)S(1)}) custom-call(f32[2,16,16,1024]{3,2,1,0:T(8,128)} %rhs_h.1, f32[16,16,1024]{2,1,0:T(8,128)} %cond_h.1, s32[16,16,1024]{2,1,0:T(8,128)} %phase_h.1, f32[32,1200]{1,0:T(8,128)} %bitcast.6, f32[8,32]{1,0:T(8,128)} %rate_h.1, f32[8,32]{1,0:T(8,128)} %gamma_h.1, ...), custom_call_target="tpu_custom_call" | custom-call | tf_op jit(solution)/shard_map/pallas_call | solution.py:632
  46.1 1.3 %copy.13 = f32[2,16,16,1024]{3,2,1,0:T(8,128)} copy(f32[2,16,16,1024]{3,2,1,0:T(8,128)S(1)} %get-tuple-element.6) | data formatting | bytes 4194304
  47.4 0.7 %copy.14 = f32[1200,32]{0,1:T(8,128)} copy(f32[1200,32]{0,1:T(8,128)S(1)} %bitcast.5) | data formatting | bytes 307200
